TPU v7x, 128 devices: a whole 4x4x4 slice. The times are simulated.
128 devices in a mesh: row: 16 (over x_lo, y, core), col: 8 (over x_hi, z).
Axes of the slice: x: 4 (x_hi: 2, x_lo: 2; x = x_hi * 2 + x_lo), y: 4, z: 4, core: 2. Of those that a mesh axis runs over, the one named last changes fastest.
Arguments:
- density: float32 [512, 12, 128, 128], P(('row', 'col')), may hold values from -0.5 to 0.5
- pattern: int32 [512, 12], replicated, may hold values from 0 to 511, as said below
- ham_strain: bfloat16 [9, 512, 12, 128, 128], P(None, ('row', 'col')), may hold values from -6 to 6
Outputs:
- purified: float32 [512, 12, 128, 128], P(('row', 'col'))
- virial: float32 [3, 3], replicated
Inputs may be any that keep to these rules, and one draw needn't show every extreme that they name: Device d = r * 8 + c holds block rows d * 4 to d * 4 + 3. Row g's pattern lists 12 distinct block rows: g itself, the other rows of its device, and one row of each of the eight devices at (r + i, c + j), i and j in -1, 0, 1, not both 0, taken modulo the grid's sizes; the order within a row is arbitrary. Together the pattern rows of one device name exactly 2 distinct rows of each of its eight neighbouring devices.
All inputs are finite; a program needn't handle non-finite values.
Results may differ from a plain program's by a relative error of at most 0.0003.
Values sent between devices are 32-bit elements; how exact they have to be, the bound alone decides.
No kernel may reach another device: no remote copies, remote signals or barrier semaphores. Data moves between devices by JAX's collectives and lax.ppermute only.
A program may use at most 256 MiB of HBM per device.

v0:
```python
import math

import jax
import jax.numpy as jnp
from jax import lax
from jax.sharding import PartitionSpec as P


def padded(value, sides, width):
    for axis, dim in sides:
        size, length = (lax.axis_size(axis), value.shape[dim])
        up = [(i, (i + 1) % size) for i in range(size)]
        down = [(j, i) for i, j in up]
        last = lax.slice_in_dim(value, length - width, length, axis=dim)
        leading = lax.slice_in_dim(value, 0, width, axis=dim)
        before = lax.ppermute(last, axis, up)
        after = lax.ppermute(leading, axis, down)
        value = jnp.concatenate([before, value, after], axis=dim)
    return value


def body(density, pattern, ham_strain):
    largest_index = lax.Precision.HIGHEST
    rows_dev = density.shape[0]
    slots = density.shape[1]
    edge = density.shape[2]
    n_row = lax.axis_size("row")
    n_col = lax.axis_size("col")
    my_row = lax.axis_index("row")
    my_col = lax.axis_index("col")
    local = jnp.arange(rows_dev, dtype=jnp.int32)
    myself = my_row % n_row * n_col + my_col % n_col
    frame = padded(density[None, None], (("row", 0), ("col", 1)), 1)
    beside_all = jnp.arange(3, dtype=jnp.int32) - 1
    frame_devs = (my_row + beside_all[:, None]) % n_row * n_col + (
        my_col + beside_all[None, :]
    ) % n_col
    frame_ids = (frame_devs[:, :, None] * rows_dev + local[None, None, :]).reshape(-1)
    count = frame_ids.shape[0]
    frame_cols = jnp.take(pattern, frame_ids, axis=0)
    mine = jnp.take(pattern, myself * rows_dev + local, axis=0)
    row_hit = frame_ids[None, None, :] == mine[:, :, None]
    col_hit = frame_cols[None, None, :, :] == mine[:, :, None, None]
    hits = row_hit[:, :, None, :, None] & col_hit[:, None, :, :, :]
    flat = (
        jnp.arange(count, dtype=jnp.int32)[:, None] * slots
        + jnp.arange(slots, dtype=jnp.int32)[None, :]
    )
    index = jnp.sum(jnp.where(hits, flat, 0), axis=(3, 4))
    found = jnp.any(hits, axis=(3, 4))
    blocks = frame.reshape(count * slots, edge, edge)
    chosen_entries = jnp.where(found[..., None, None], jnp.take(blocks, index, axis=0), 0.0)
    squared_density = jnp.einsum(
        "isab,istbc->itac", density, chosen_entries, precision=largest_index
    )
    cubed_density = jnp.einsum(
        "isab,istbc->itac", squared_density, chosen_entries, precision=largest_index
    )
    purified = 3.0 * squared_density - 2.0 * cubed_density
    total_blocks = rows_dev * n_row * n_col
    factor = 1.0 / math.sqrt(float(total_blocks * slots * edge * edge))
    parts = jnp.stack(
        [jnp.sum(ham_strain[comp].astype(jnp.float32) * purified) for comp in range(9)]
    )
    summed = lax.psum(parts, ("row", "col"))
    virial = (summed * factor).reshape(3, 3)
    return (purified, virial)


def solution(mesh):
    in_specs = (P(("row", "col"), None, None, None), P(), P(None, ("row", "col"), None, None, None))
    out_specs = (P(("row", "col"), None, None, None), P())
    return jax.shard_map(body, mesh=mesh, in_specs=in_specs, out_specs=out_specs, check_vma=False)
```

profile of v0, /device:TPU:1, one launch (start us, length us, event | category | flops | bytes accessed | tf_op | source)
XLA Modules:
  0.0 516.8 jit_solution(4297540789362770055)
XLA Ops:
  0.6 1.5 collective-permute-start.1
  2.1 1.3 collective-permute-start
  3.5 35.4 %collective-permute-done.1 = f32[1,1,4,12,128,128]{5,4,3,2,1,0:T(8,128)S(1)} collective-permute-done((f32[1,1,4,12,128,128]{5,4,3,2,1,0:T(8,128)}, f32[1,1,4,12,128,128]{5,4,3,2,1,0:T(8,128)S(1)}, u32[]{:S(2)}, u32[]{:S(2)}) %collective-permute-start.1) | collective-permute-done | bytes 3145760 | tf_op jit(solution)/shard_map/ppermute | solution.py:17
  38.9 8.8 %pad_maximum_fusion.1 = f32[3,1,4,12,128,128]{5,4,3,2,1,0:T(8,128)} fusion(f32[1,1,4,12,128,128]{5,4,3,2,1,0:T(8,128)S(1)} %collective-permute-done.1, f32[1,1,4,12,128,128]{5,4,3,2,1,0:T(8,128)} %bitcast.94, f32[1,1,4,12,128,128]{5,4,3,2,1,0:T(8,128)S(1)} %collective-permute-done), kind=kLoop, calls=%fused_computation.15 | loop fusion | flops 4718592 | bytes 18874368 | tf_op jit(solution)/shard_map/concatenate | solution.py:18
  47.7 6.2 %collective-permute-start.3 = (f32[3,1,4,12,128,128]{5,4,3,2,1,0:T(8,128)}, f32[3,1,4,12,128,128]{5,4,3,2,1,0:T(8,128)}, u32[]{:S(2)}, u32[]{:S(2)}) collective-permute-start(f32[3,1,4,12,128,128]{5,4,3,2,1,0:T(8,128)} %pad_maximum_fusion.1), channel_id=1, source_target_pairs={{1,0},{2,1},{3,2},{4,3},{5,4},{6,5},{7,6},{0,7},{9,8},{10,9},{11,1... | collective-permute-start | bytes 28311560 | tf_op jit(solution)/shard_map/ppermute | solution.py:17
  54.4 0.6 gather_fusion
  55.0 0.6 gather_fusion.1
  56.2 2.6 and_reduce_fusion
  58.8 0.2 copy.38
  59.0 2.5 fusion.10
  61.6 0.2 copy.39
  61.8 0.2 copy.40
  62.1 10.2 %fusion.35 = (bf16[1,4,12,128,128]{4,3,2,1,0:T(8,128)(2,1)}, bf16[1,4,12,128,128]{4,3,2,1,0:T(8,128)(2,1)}, bf16[1,4,12,128,128]{4,3,2,1,0:T(8,128)(2,1)}, bf16[...) fusion(bf16[9,4,12,128,128]{4,3,2,1,0:T(8,128)(2,1)} %param.5), kind=kLoop, calls=%fused_computation.80 | loop fusion | bytes 28311552 | tf_op jit(solution)/shard_map/slice | solution.py:63
  72.3 2.6 copy.64
  74.9 2.6 copy.71
  77.5 2.6 copy.70
  80.1 2.6 copy.69
  82.6 2.6 copy.68
  85.3 1.6 copy.67
  86.8 1.6 copy.66
  88.5 2.7 copy.65
  91.2 2.6 copy.72
  93.8 158.3 %collective-permute-done.3 = f32[3,1,4,12,128,128]{5,4,3,2,1,0:T(8,128)} collective-permute-done((f32[3,1,4,12,128,128]{5,4,3,2,1,0:T(8,128)}, f32[3,1,4,12,128,128]{5,4,3,2,1,0:T(8,128)}, u32[]{:S(2)}, u32[]{:S(2)}) %collective-permute-start.3) | collective-permute-done | bytes 9437216 | tf_op jit(solution)/shard_map/ppermute | solution.py:17
  252.1 5.5 %collective-permute-done.2 = f32[3,1,4,12,128,128]{5,4,3,2,1,0:T(8,128)} collective-permute-done((f32[3,1,4,12,128,128]{5,4,3,2,1,0:T(8,128)}, f32[3,1,4,12,128,128]{5,4,3,2,1,0:T(8,128)}, u32[]{:S(2)}, u32[]{:S(2)}) %collective-permute-start.2) | collective-permute-done | bytes 9437216 | tf_op jit(solution)/shard_map/ppermute | solution.py:16
  257.6 19.4 %pad_maximum_fusion = f32[3,3,4,12,128,128]{5,4,3,2,1,0:T(8,128)} fusion(f32[3,1,4,12,128,128]{5,4,3,2,1,0:T(8,128)} %collective-permute-done.3, f32[1,1,4,12,128,128]{5,4,3,2,1,0:T(8,128)} %copy-done.1, f32[1,1,4,12,128,128]{5,4,3,2,1,0:T(8,128)S(1)} %bitcast.95, f32[1,1,4,12,128,128]{5,4,3,2,1,0:T(8,128)} %copy-done.2, ...), kind=kLoop, calls=%fused_computation.6 | loop fusion | flops 28311552 | bytes 56623104 | tf_op jit(solution)/shard_map/concatenate | solution.py:18
  277.0 28.4 %gather_fusion.2 = f32[576,128,128]{2,1,0:T(8,128)} fusion(f32[432,128,128]{2,1,0:T(8,128)} %bitcast.89, s32[1024]{0:T(1024)S(1)} %pad_clamp_fusion), kind=kCustom, calls=%fused_computation.2 | custom fusion | bytes 75499776 | tf_op jit(solution)/shard_map/jit(_take)/gather | solution.py:52
  305.5 65.1 %fusion = f32[4,12,128,128,1]{3,2,1,4,0:T(8,128)S(1)} fusion(f32[4,12,12,128,128]{4,3,2,1,0:T(8,128)} %bitcast.90, pred[4,12,12]{2,1,0:T(8,128)(4,1)S(1)} %copy.39, pred[4,12,12]{2,1,0:T(8,128)(4,1)S(1)} %copy.38, f32[4,12,128,128]{3,2,1,0:T(8,128)S(1)} %copy-done), kind=kOutput, calls=%fused_computation.4 | convolution fusion | flops 14514388992 | bytes 44041344 | tf_op jit(solution)/shard_map/isab,istbc->itac/dot_general | solution.py:53
  370.6 68.0 %fusion.15 = (f32[]{:T(128)}, f32[]{:T(128)}, f32[]{:T(128)}, f32[]{:T(128)}, f32[]{:T(128)}, /*index=5*/f32[]{:T(128)}, f32[]{:T(128)}, f32[]{:T(128)}, f32[]{:T(128)}, f32[4,12,128,128]{2,3,1,0:T(8,128)S(1)}) fusion(bf16[1,4,12,128,128]{3,4,2,1,0:T(8,128)(2,1)} %copy.72, bf16[1,4,12,128,128]{3,4,2,1,0:T(8,128)(2,1)S(1)} %copy-done.4, ...), kind=kOutput, calls=%fused_computation.26 | convolution fusion | flops 14537981952 | bytes 58197156 | tf_op jit(solution)/shard_map/isab,istbc->itac/dot_general | solution.py:56
  438.6 5.7 %stack.39 = f32[9]{0:T(128)S(1)} concatenate(f32[1]{0:T(128)} %bitcast.17, f32[1]{0:T(128)} %bitcast.19, f32[1]{0:T(128)} %bitcast.21, f32[1]{0:T(128)} %bitcast.23, f32[1]{0:T(128)} %bitcast.25, f32[1]{0:T(128)} %bitcast.27, f32[1]{0:T(128)} %bitcast.29, f32[1]{0:T(128)} %bitcast.31, f32[1]{0:T(128)} %bitcast.33), dimensions={0} | concatenate | bytes 72 | tf_op jit(solution)/shard_map/stack | solution.py:62
  444.3 2.4 copy.53
  446.6 69.1 %psum.7 = f32[9]{0:T(128)S(1)} all-reduce(f32[9]{0:T(128)S(1)} %stack.39), channel_id=1, replica_groups=mesh['row'=16,'col'=8] {'row','col'}, use_global_device_ids=true, to_apply=%region_11.12 | all-reduce | flops 9 | bytes 72 | tf_op jit(solution)/shard_map/psum | solution.py:65
  515.7 0.7 reshape.249
  (45 shorter events, 1.3 us)
Async XLA Ops:
  0.6 53.6 %copy-start.8 = (s32[512,12]{0,1:T(8,128)S(1)}, s32[512,12]{0,1:T(8,128)}, u32[]{:S(2)}) copy-start(s32[512,12]{0,1:T(8,128)} %param.4) | copy-start | bytes 73732
  0.6 38.2 %collective-permute-start.1 = (f32[1,1,4,12,128,128]{5,4,3,2,1,0:T(8,128)}, f32[1,1,4,12,128,128]{5,4,3,2,1,0:T(8,128)S(1)}, u32[]{:S(2)}, u32[]{:S(2)}) collective-permute-start(f32[1,1,4,12,128,128]{5,4,3,2,1,0:T(8,128)} %bitcast.92), channel_id=1, source_target_pairs={{8,0},{16,8},{24,16},{32,24},{40,32},{48,40},{56,48},{64,56},{72,6... | collective-permute-start | bytes 9437192 | tf_op jit(solution)/shard_map/ppermute | solution.py:17
  2.1 36.7 %collective-permute-start = (f32[1,1,4,12,128,128]{5,4,3,2,1,0:T(8,128)}, f32[1,1,4,12,128,128]{5,4,3,2,1,0:T(8,128)S(1)}, u32[]{:S(2)}, u32[]{:S(2)}) collective-permute-start(f32[1,1,4,12,128,128]{5,4,3,2,1,0:T(8,128)} %bitcast.93), channel_id=1, source_target_pairs={{0,8},{8,16},{16,24},{24,32},{32,40},{40,48},{48,56},{56,64},{64,7... | collective-permute-start | bytes 9437192 | tf_op jit(solution)/shard_map/ppermute | solution.py:16
  38.9 8.8 %copy-start.1 = (f32[1,1,4,12,128,128]{5,4,3,2,1,0:T(8,128)}, f32[1,1,4,12,128,128]{5,4,3,2,1,0:T(8,128)S(1)}, u32[]{:S(2)}) copy-start(f32[1,1,4,12,128,128]{5,4,3,2,1,0:T(8,128)S(1)} %collective-permute-done.1) | copy-start | bytes 9437188
  38.9 8.8 %copy-start.2 = (f32[1,1,4,12,128,128]{5,4,3,2,1,0:T(8,128)}, f32[1,1,4,12,128,128]{5,4,3,2,1,0:T(8,128)S(1)}, u32[]{:S(2)}) copy-start(f32[1,1,4,12,128,128]{5,4,3,2,1,0:T(8,128)S(1)} %collective-permute-done) | copy-start | bytes 9437188
  47.7 204.4 %collective-permute-start.3 = (f32[3,1,4,12,128,128]{5,4,3,2,1,0:T(8,128)}, f32[3,1,4,12,128,128]{5,4,3,2,1,0:T(8,128)}, u32[]{:S(2)}, u32[]{:S(2)}) collective-permute-start(f32[3,1,4,12,128,128]{5,4,3,2,1,0:T(8,128)} %pad_maximum_fusion.1), channel_id=1, source_target_pairs={{1,0},{2,1},{3,2},{4,3},{5,4},{6,5},{7,6},{0,7},{9,8},{10,9},{11,1... | collective-permute-start | bytes 28311560 | tf_op jit(solution)/shard_map/ppermute | solution.py:17
  53.9 203.8 %collective-permute-start.2 = (f32[3,1,4,12,128,128]{5,4,3,2,1,0:T(8,128)}, f32[3,1,4,12,128,128]{5,4,3,2,1,0:T(8,128)}, u32[]{:S(2)}, u32[]{:S(2)}) collective-permute-start(f32[3,1,4,12,128,128]{5,4,3,2,1,0:T(8,128)} %pad_maximum_fusion.1), channel_id=1, source_target_pairs={{0,1},{1,2},{2,3},{3,4},{4,5},{5,6},{6,7},{7,0},{8,9},{9,10},{10,1... | collective-permute-start | bytes 28311560 | tf_op jit(solution)/shard_map/ppermute | solution.py:16
  88.5 169.2 %copy-start = (f32[4,12,128,128]{3,2,1,0:T(8,128)S(1)}, f32[4,12,128,128]{3,2,1,0:T(8,128)}, u32[]{:S(2)}) copy-start(f32[4,12,128,128]{3,2,1,0:T(8,128)} %param.3) | copy-start | bytes 9437188
  305.5 65.1 %copy-start.3 = (bf16[1,4,12,128,128]{3,4,2,1,0:T(8,128)(2,1)S(1)}, bf16[1,4,12,128,128]{3,4,2,1,0:T(8,128)(2,1)}, u32[]{:S(2)}) copy-start(bf16[1,4,12,128,128]{3,4,2,1,0:T(8,128)(2,1)} %copy.64) | copy-start | bytes 4718596
  305.5 65.1 %copy-start.4 = (bf16[1,4,12,128,128]{3,4,2,1,0:T(8,128)(2,1)S(1)}, bf16[1,4,12,128,128]{3,4,2,1,0:T(8,128)(2,1)}, u32[]{:S(2)}) copy-start(bf16[1,4,12,128,128]{3,4,2,1,0:T(8,128)(2,1)} %copy.71) | copy-start | bytes 4718596
  305.5 65.1 %copy-start.5 = (bf16[1,4,12,128,128]{3,4,2,1,0:T(8,128)(2,1)S(1)}, bf16[1,4,12,128,128]{3,4,2,1,0:T(8,128)(2,1)}, u32[]{:S(2)}) copy-start(bf16[1,4,12,128,128]{3,4,2,1,0:T(8,128)(2,1)} %copy.70) | copy-start | bytes 4718596
  305.5 65.1 %copy-start.6 = (bf16[1,4,12,128,128]{3,4,2,1,0:T(8,128)(2,1)S(1)}, bf16[1,4,12,128,128]{3,4,2,1,0:T(8,128)(2,1)}, u32[]{:S(2)}) copy-start(bf16[1,4,12,128,128]{3,4,2,1,0:T(8,128)(2,1)} %copy.69) | copy-start | bytes 4718596
  305.5 65.2 %copy-start.7 = (bf16[1,4,12,128,128]{3,4,2,1,0:T(8,128)(2,1)S(1)}, bf16[1,4,12,128,128]{3,4,2,1,0:T(8,128)(2,1)}, u32[]{:S(2)}) copy-start(bf16[1,4,12,128,128]{3,4,2,1,0:T(8,128)(2,1)} %copy.68) | copy-start | bytes 4718596
where the time goes:
time: 523 us; the launch traced here: 517 us
  waiting for transfers between devices  199 us (38%)
  matrix products  133 us (25%)
  local copies, waits for them, and re-layouts  71.2 us (14%)
  blocking collectives  69.1 us (13%)
  other arithmetic  33.9 us (6%)
  starting transfers between devices  9.06 us (2%)
    ppermute x2, waiting for transfers between devices, padded(): after = lax.ppermute(leading, axis, down)  194 us
    psum x1, blocking collectives, body(): summed = lax.psum(parts, ('row', 'col'))  69.1 us
    dot_general x1, matrix products, body(): jnp.einsum('isab,istbc->itac', squared_density, chosen_entries, precision...  68 us
    dot_general x1, matrix products, body(): jnp.einsum('isab,istbc->itac', density, chosen_entries, precision=largest...  65.1 us
    gather x1, local copies, waits for them, and re-layouts, body(): jnp.take(blocks, index, axis=0)  28.4 us
    concatenate x2, other arithmetic, padded(): value = jnp.concatenate([before, value, after], axis=dim)  28.2 us
    unnamed x29, local copies, waits for them, and re-layouts  24.1 us
  transfers between devices with their start and end apart: 4, of which 3 were waited for; matrix products, arithmetic and copies ran while one was open for 8% of the time, Pallas kernels for 0%

commit v1 on v0

v1 whole, which is shorter than its diff:
```python
import math

import jax
import jax.numpy as jnp
from jax import lax
from jax.experimental import pallas as pl
from jax.experimental.pallas import tpu as pltpu
from jax.sharding import PartitionSpec as P

AXES = ("row", "col")
EDGE = 128
OWN = 4
SLOTS = 12
N_ROW = 16
N_COL = 8
N_DEV = N_ROW * N_COL

DIRS = ((-1, -1), (-1, 0), (-1, 1), (0, -1), (0, 1), (1, -1), (1, 0), (1, 1))


def near(a, b):
    return max(abs(a[0] - b[0]), abs(a[1] - b[1])) <= 1


COMMON = tuple(
    tuple(e for e in range(8) if e != d and near(DIRS[e], DIRS[d])) for d in range(8)
)
COUNT = tuple(2 + len(COMMON[d]) for d in range(8))
BACK = tuple(DIRS.index((dr, -dc)) for dr, dc in DIRS)
SEEN = tuple(
    tuple(
        DIRS.index(
            (
                (DIRS[e][0] - DIRS[d][0]) * (1 if DIRS[d][0] == 0 else -1),
                DIRS[e][1] - DIRS[d][1],
            )
        )
        for e in COMMON[d]
    )
    for d in range(8)
)

T_SLOT = 0
T_NAME = 48
T_LOW = 96
T_FAR = 104
T_SEND = 264
T_SIZE = 264 + 80
SEND_AT = tuple(T_SEND + 2 * sum(COUNT[:f]) for f in range(8))
CODES = tuple((dr + 1) * 3 + dc + 1 for dr, dc in DIRS)


def place(value, row, col):
    dev = value >> 2
    dr = ((dev >> 3) - row + 1) & (N_ROW - 1)
    dc = ((dev & (N_COL - 1)) - col + 1) & (N_COL - 1)
    return jnp.where(((row & 1) == 1) & (dr < 3), 2 - dr, dr), dc


def device_at(row, col, d):
    dr, dc = DIRS[d]
    towards = 1 - 2 * (row & 1)
    return ((row + dr * towards) & (N_ROW - 1)) * N_COL + ((col + dc) & (N_COL - 1))


def own_table(pat, row, col, tab):
    me = row * N_COL + col
    for l in range(OWN):
        for u in range(SLOTS):
            value = pat[u, me * OWN + l]
            dr, dc = place(value, row, col)
            code = dr * 3 + dc
            number = value & 3
            o = jnp.where(code == 4, number, code + jnp.where(code > 4, 3, 4))
            tab[T_SLOT + l * SLOTS + o] = u
            tab[T_NAME + l * SLOTS + o] = number


def named_rows(pat, other, me):
    named = []
    for j in range(OWN):
        number = jnp.int32(0)
        for u in range(SLOTS):
            value = pat[u, other * OWN + j]
            number = jnp.where((value >> 2) == me, value & 3, number)
        named.append(number)
    low = jnp.minimum(jnp.minimum(named[0], named[1]), jnp.minimum(named[2], named[3]))
    high = jnp.maximum(jnp.maximum(named[0], named[1]), jnp.maximum(named[2], named[3]))
    return low, high


def send_table(pat, row, col, tab):
    for f in range(8):
        d = BACK[f]
        rows = named_rows(pat, device_at(row, col, f), row * N_COL + col)
        for k, l in enumerate(rows):
            columns = [l, 4 + f] + [4 + e for e in SEEN[d]]
            for m, o in enumerate(columns):
                tab[SEND_AT[f] + k * COUNT[d] + m] = l * SLOTS + tab[T_SLOT + l * SLOTS + o]


def own_of(tab, f, k):
    return tab[SEND_AT[f] + k * COUNT[f] + 1]


def rest_of(tab, f, k):
    at = SEND_AT[f] + k * COUNT[f]
    return [tab[at]] + [tab[at + m] for m in range(2, COUNT[f])]


def fill(out, tab, dens, f):
    for k in range(2):
        out[k] = dens[own_of(tab, f, k)]
        for m, n in enumerate(rest_of(tab, f, k)):
            out[2 + k * (COUNT[f] - 1) + m] = dens[n]


def first_kernel(pat_in, dens_in, dens, tab, near_m, near_p, far_m, far_p, beside, pat, sem):
    load = pltpu.make_async_copy(dens_in, dens, sem.at[0])
    load.start()
    pat_load = pltpu.make_async_copy(pat_in, pat, sem.at[1])
    pat_load.start()
    pat_load.wait()
    row = lax.axis_index("row")
    col = lax.axis_index("col")
    own_table(pat, row, col, tab)
    send_table(pat, row, col, tab)
    load.wait()
    for out, f, edge in ((near_m, 5, 3), (near_p, 7, 4)):
        fill(out, tab, dens, f)
        for k in range(2):
            out[8 + k] = dens[own_of(tab, edge, k)]
    for out, f in ((far_m, 0), (far_p, 2), (beside, 1)):
        fill(out, tab, dens, f)


def second_kernel(tab, dens, behind, ahead, *refs):
    pair, late_m, late_p = refs[4:]
    fill(pair, tab, dens, 6)
    for k in range(2):
        pair[12 + k] = behind[8 + k]
        pair[14 + k] = ahead[8 + k]
    for f, out in ((3, late_m), (4, late_p)):
        for k in range(2):
            for m, n in enumerate(rest_of(tab, f, k)):
                out[5 * k + m] = dens[n]


def far_table(pat, row, col, tab):
    for d in range(8):
        names = [tab[T_NAME + l * SLOTS + 4 + d] for l in range(OWN)]
        low = jnp.minimum(jnp.minimum(names[0], names[1]), jnp.minimum(names[2], names[3]))
        high = jnp.maximum(jnp.maximum(names[0], names[1]), jnp.maximum(names[2], names[3]))
        tab[T_LOW + d] = low
        other = device_at(row, col, d)
        for k, l in enumerate((low, high)):
            for u in range(SLOTS):
                value = pat[u, other * OWN + l]
                dr, dc = place(value, row, col)
                code = jnp.where((dr < 3) & (dc < 3), dr * 3 + dc, 9)
                tab[T_FAR + (2 * d + k) * 10 + code] = value & 3


def split(value):
    high = value.astype(jnp.bfloat16)
    low = (value - high.astype(jnp.float32)).astype(jnp.bfloat16)
    return jnp.concatenate([high, low], axis=1)


def product(left, right):
    return jnp.dot(
        left, jnp.concatenate([right, right], axis=0), preferred_element_type=jnp.float32
    )


def halves(value):
    return value[:, :EDGE] + value[:, EDGE:]


def bit(tab, g, d):
    return jnp.where(tab[T_NAME + g * SLOTS + 4 + d] == tab[T_LOW + d], 0, 1)


def local_kernel(pat, dens, tab_in, ham, tab, wide, square, ham_out, zeros, sem):
    for c in range(9):
        pltpu.make_async_copy(ham.at[c], ham_out.at[c], sem.at[c]).start()
    row = lax.axis_index("row")
    col = lax.axis_index("col")
    for i in range(T_LOW):
        tab[i] = tab_in[i]
    for i in range(T_SEND, T_SIZE):
        tab[i] = tab_in[i]
    far_table(pat, row, col, tab)
    zeros[...] = jnp.zeros_like(zeros)

    def widen(i, _):
        wide[i] = split(dens[i // SLOTS * SLOTS + tab[T_SLOT + i]])
        return 0

    lax.fori_loop(0, OWN * SLOTS, widen, 0)

    def rows(g, _):
        for t in range(SLOTS):
            total = None
            for s in range(OWN):
                left = wide[g * SLOTS + s]
                if t >= OWN:
                    left = masked(same_name(tab, g, s, t), left, zeros)
                total = add(total, product(left, wide[s * SLOTS + t]))
            square[g * SLOTS + t] = halves(total)
        return 0

    lax.fori_loop(0, OWN, rows, 0)
    for c in range(9):
        pltpu.make_async_copy(ham.at[c], ham_out.at[c], sem.at[c]).wait()


def masked(match, left, zeros):
    if match is None:
        return left
    return jnp.where(match, left, zeros[...])


def same_name(tab, g, s, o):
    return bit(tab, g, o - OWN) == bit(tab, s, o - OWN)


def add(total, term):
    return term if total is None else total + term


def own_terms(tab, g, dirs):
    out = []
    for d in dirs:
        b = bit(tab, g, d)
        out.append((4 + d, tab[T_FAR + (2 * d + b) * 10 + 4], 2 * d + b))
    return out


def far_terms(tab, g, dirs, at, terms):
    for d in dirs:
        b = bit(tab, g, d)
        base = at[d] + b * (COUNT[d] - 1)
        info = T_FAR + (2 * d + b) * 10
        terms[4 + d].append((4 + d, None, base))
        for j, e in enumerate(COMMON[d]):
            match = tab[info + CODES[e]] == tab[T_NAME + g * SLOTS + 4 + e]
            terms[4 + e].append((4 + d, match, base + 1 + j))
    return terms


def no_terms():
    return {o: [] for o in range(OWN, SLOTS)}


def offsets(dirs):
    out, total = {}, 0
    for d in dirs:
        out[d] = total
        total += 2 * (COUNT[d] - 1)
    return out, total


EARLY = (0, 1, 2, 5, 7)
PAIR = (6,)
LATE = (3, 4)
EARLY_AT, N_EARLY = offsets(EARLY)
PAIR_AT, N_PAIR = offsets(PAIR)
LATE_AT, N_LATE = offsets(LATE)


def widen(ref, start, out, at, count):
    def one(i, _):
        out[at + i] = split(ref[start + i])
        return 0

    lax.fori_loop(0, count, one, 0, unroll=2)


def chain(total, listed, lefts, rights, zeros):
    for left, match, index in listed:
        total = add(total, product(masked(match, lefts(left), zeros), rights[index]))
    return total


def early_kernel(tab, wide, square_in, near_m, near_p, far_m, far_p, beside, after, also,
                 own, early, square, back_buf, zeros):
    del after, also
    zeros[...] = jnp.zeros_like(zeros)
    for d, ref in ((0, far_m), (1, beside), (2, far_p), (5, near_m), (7, near_p)):
        for k in range(2):
            own[2 * d + k] = split(ref[k])
        widen(ref, 2, early, EARLY_AT[d], 2 * (COUNT[d] - 1))

    def rows(g, _):
        back = own_terms(tab, g, EARLY)
        terms = far_terms(tab, g, EARLY, EARLY_AT, no_terms())
        lefts = lambda left: wide[g * SLOTS + left]
        for i, (left, number, index) in enumerate(back):
            back_buf[i] = halves(product(lefts(left), own[index]))
        for o in range(SLOTS):
            value = square_in[g * SLOTS + o]
            if o >= OWN and terms[o]:
                value = value + halves(chain(None, terms[o], lefts, early, zeros))
            square[g * SLOTS + o] = value
        for i, (left, number, index) in enumerate(back):
            square[g * SLOTS + number] = square[g * SLOTS + number] + back_buf[i]
        return 0

    lax.fori_loop(0, OWN, rows, 0)


def pair_kernel(tab, wide, square_in, pair_in, own, pair, square, cube, back_buf, wsq, zeros):
    zeros[...] = jnp.zeros_like(zeros)
    for d, start in ((6, 0), (3, 12), (4, 14)):
        for k in range(2):
            own[2 * d + k] = split(pair_in[start + k])
    widen(pair_in, 2, pair, 0, N_PAIR)

    def rows(g, _):
        back = own_terms(tab, g, PAIR + LATE)
        terms = far_terms(tab, g, PAIR, PAIR_AT, no_terms())
        lefts = lambda left: wide[g * SLOTS + left]
        for i, (left, number, index) in enumerate(back):
            back_buf[i] = halves(product(lefts(left), own[index]))
        for o in range(SLOTS):
            value = square_in[g * SLOTS + o]
            if o >= OWN and terms[o]:
                value = value + halves(chain(None, terms[o], lefts, pair, zeros))
            square[g * SLOTS + o] = value
        for i, (left, number, index) in enumerate(back):
            square[g * SLOTS + number] = square[g * SLOTS + number] + back_buf[i]
        for o in range(OWN):
            wsq[o] = split(square[g * SLOTS + o])
        for o in range(SLOTS):
            total = None
            for s in range(OWN):
                left = wsq[s]
                if o >= OWN:
                    left = masked(same_name(tab, g, s, o), left, zeros)
                total = add(total, product(left, wide[s * SLOTS + o]))
            cube[g * SLOTS + o] = halves(total)
        return 0

    lax.fori_loop(0, OWN, rows, 0)


def final_kernel(tab, wide, own_early, own_late, early, pair, square, cube, behind, ahead, ham,
                 purified, virial, late, far_square, wsq, own_cube, out_buf, sums, zeros, out_sem):
    zeros[...] = jnp.zeros_like(zeros)
    sums[...] = jnp.zeros_like(sums)
    for d, ref in ((3, behind), (4, ahead)):
        widen(ref, 0, late, LATE_AT[d], 10)

    def rows(g, _):
        late_terms = far_terms(tab, g, LATE, LATE_AT, no_terms())
        pair_terms = far_terms(tab, g, PAIR, PAIR_AT, no_terms())
        early_terms = far_terms(tab, g, EARLY, EARLY_AT, no_terms())
        lefts = lambda left: wide[g * SLOTS + left]
        for o in range(OWN, SLOTS):
            total = chain(None, late_terms[o], lefts, late, zeros)
            value = square[g * SLOTS + o] + halves(total)
            far_square[o - OWN] = value
            wsq[o - OWN] = split(value)

        def finish(o, value):
            slot = tab[T_SLOT + g * SLOTS + o]
            out_buf[g, slot] = value
            for c in range(9):
                part = ham[c, g, slot].astype(jnp.float32) * value
                sums[c] += jnp.sum(part.reshape(EDGE // 8, 8, EDGE), axis=0)

        lefts = lambda left: wsq[left - OWN]
        for o in range(OWN):
            own_cube[o] = cube[g * SLOTS + o]
        for dirs, own in ((EARLY, own_early), (PAIR + LATE, own_late)):
            for left, number, index in own_terms(tab, g, dirs):
                term = halves(product(lefts(left), own[index]))
                own_cube[number] = own_cube[number] + term
        for o in range(OWN, SLOTS):
            total = chain(None, pair_terms[o], lefts, pair, zeros)
            total = chain(total, early_terms[o], lefts, early, zeros)
            total = chain(total, late_terms[o], lefts, late, zeros)
            finish(o, 3.0 * far_square[o - OWN] - 2.0 * (cube[g * SLOTS + o] + halves(total)))
        for o in range(OWN):
            finish(o, 3.0 * square[g * SLOTS + o] - 2.0 * own_cube[o])
        pltpu.make_async_copy(out_buf.at[g], purified.at[g], out_sem.at[g]).start()
        return 0

    lax.fori_loop(0, OWN, rows, 0)
    lane = lax.broadcasted_iota(jnp.int32, (8, EDGE), 1)
    line = jnp.zeros((8, EDGE), jnp.float32)
    for c in range(9):
        line = jnp.where(lane == c, jnp.sum(sums[c]), line)
    for i in range(N_DEV // 8):
        virial[pl.ds(i * 8, 8)] = line
    for g in range(OWN):
        pltpu.make_async_copy(out_buf.at[g], purified.at[g], out_sem.at[g]).wait()


def from_direction(d):
    dr, dc = DIRS[d]
    pairs = []
    for row in range(N_ROW):
        for col in range(N_COL):
            towards = 1 - 2 * (row & 1)
            there = (row + dr * towards) % N_ROW * N_COL + (col + dc) % N_COL
            pairs.append((there, row * N_COL + col))
    return pairs


ANY = pl.BlockSpec(memory_space=pl.ANY)
VMEM = pl.BlockSpec(memory_space=pltpu.VMEM)
SMEM = pl.BlockSpec(memory_space=pltpu.SMEM)
HBM = pl.BlockSpec(memory_space=pltpu.HBM)
F32 = jnp.float32
BF16 = jnp.bfloat16


def call(kernel, name, out, in_specs, out_specs, scratch, flops, moved, vmem=32):
    return pl.pallas_call(
        kernel,
        out_shape=out,
        in_specs=in_specs,
        out_specs=out_specs,
        scratch_shapes=scratch,
        compiler_params=pltpu.CompilerParams(vmem_limit_bytes=vmem << 20),
        cost_estimate=pl.CostEstimate(
            flops=flops * 2 * 4 * EDGE**3, bytes_accessed=moved << 20, transcendentals=0
        ),
        name=name,
    )


def blocks(*lead):
    return jax.ShapeDtypeStruct(lead + (EDGE, EDGE), F32)


def wides(*lead):
    return jax.ShapeDtypeStruct(lead + (EDGE, 2 * EDGE), BF16)


def wide_scratch(*lead):
    return pltpu.VMEM(lead + (EDGE, 2 * EDGE), BF16)


def scratch(*lead):
    return pltpu.VMEM(lead + (EDGE, EDGE), F32)


def body(density, pattern, ham_strain):
    dma = pltpu.SemaphoreType.DMA
    table = jax.ShapeDtypeStruct((T_SIZE,), jnp.int32)
    dens, tab, near_m, near_p, far_m, far_p, beside = call(
        first_kernel, "first",
        (blocks(OWN * SLOTS), table, blocks(10), blocks(10), blocks(8), blocks(8), blocks(12)),
        [HBM, HBM], (VMEM, SMEM) + (VMEM,) * 5,
        [pltpu.SMEM((SLOTS, N_DEV * OWN), jnp.int32), dma((2,))], 0, 10, 53,
    )(pattern.T, density.reshape(OWN * SLOTS, EDGE, EDGE))
    near_ahead = lax.ppermute(near_m, AXES, from_direction(7))
    near_behind = lax.ppermute(near_p, AXES, from_direction(5))
    far_ahead = lax.ppermute(far_m, AXES, from_direction(2))
    far_behind = lax.ppermute(far_p, AXES, from_direction(0))
    beside = lax.ppermute(beside, AXES, from_direction(1))
    tab, wide, square, ham = call(
        local_kernel, "local",
        (table, wides(OWN * SLOTS), blocks(OWN * SLOTS),
         jax.ShapeDtypeStruct(ham_strain.shape, BF16)),
        [SMEM, VMEM, SMEM, HBM], (SMEM, VMEM, VMEM, VMEM), [wide_scratch(), dma((9,))], 192, 36,
    )(pattern.T, dens, tab, ham_strain)
    pair, late_m, late_p = call(
        second_kernel, "second", (blocks(16), blocks(10), blocks(10)),
        [SMEM] + [VMEM] * 3 + [ANY] * 4, (VMEM,) * 3, [], 0, 4,
    )(tab, dens, near_behind, near_ahead, far_behind, far_ahead, beside, square)
    late_ahead = lax.ppermute(late_m, AXES, from_direction(4))
    late_behind = lax.ppermute(late_p, AXES, from_direction(3))
    pair_in = lax.ppermute(pair, AXES, from_direction(6))
    own_early, early, square = call(
        early_kernel, "early",
        (wides(16), wides(N_EARLY), blocks(OWN * SLOTS)),
        [SMEM] + [VMEM] * 7 + [ANY] * 2, (VMEM,) * 3,
        [scratch(8), wide_scratch()], 88, 10,
    )(tab, wide, square, near_behind, near_ahead, far_behind, far_ahead, beside, pair, late_m)
    own_late, pair, square, cube = call(
        pair_kernel, "pair",
        (wides(16), wides(N_PAIR), blocks(OWN * SLOTS), blocks(OWN * SLOTS)),
        [SMEM] + [VMEM] * 3, (VMEM,) * 4,
        [scratch(8), wide_scratch(OWN), wide_scratch()], 224, 10,
    )(tab, wide, square, pair_in)
    purified, line = call(
        final_kernel, "final",
        (blocks(OWN, SLOTS), jax.ShapeDtypeStruct((N_DEV, EDGE), F32)),
        [SMEM] + [VMEM] * 10, (ANY, VMEM),
        [
            wide_scratch(N_LATE), scratch(8), wide_scratch(8), scratch(OWN),
            scratch(OWN, SLOTS), pltpu.VMEM((9, 8, EDGE), F32), wide_scratch(), dma((OWN,)),
        ], 200, 30,
    )(tab, wide, own_early, own_late, early, pair, square, cube, late_behind, late_ahead, ham)
    total_blocks = N_DEV * OWN
    factor = 1.0 / math.sqrt(float(total_blocks * SLOTS * EDGE * EDGE))
    lines = lax.all_to_all(line, AXES, 0, 0, tiled=True)
    virial = (jnp.sum(lines, axis=0)[:9] * factor).reshape(3, 3)
    return purified, virial


def solution(mesh):
    in_specs = (P(AXES, None, None, None), P(), P(None, AXES, None, None, None))
    out_specs = (P(AXES, None, None, None), P())
    return jax.shard_map(body, mesh=mesh, in_specs=in_specs, out_specs=out_specs, check_vma=False)
```

time: 523 us -> 102 us (0.20); the launches traced: 517 us -> 102 us
  waiting for transfers between devices: 199 us -> 12.8 us
  matrix products: 133 us -> 0 us
  local copies, waits for them, and re-layouts: 71.2 us -> 3.31 us
  blocking collectives: 69.1 us -> 17.2 us
  Pallas kernels: 0 us -> 41.5 us
  other arithmetic: 33.9 us -> 0.16 us
  starting transfers between devices: 9.06 us -> 26.3 us
    ppermute x4 -> x8, waiting for transfers between devices: 199 us -> 12.8 us  [the longest x1 5.15 us: body(): late_behind = lax.ppermute(late_p, AXES, from_direction(3))]
    dot_general x2 -> x0, matrix products: 133 us -> none  [the longest x1 68 us: body(): jnp.einsum('isab,istbc->itac', squared_density, chosen_entries, precision...]
    psum x1 -> x0, blocking collectives: 69.1 us -> none  [body(): summed = lax.psum(parts, ('row', 'col'))]
    pallas_call x0 -> x6, Pallas kernels: none -> 41.5 us  [the longest x1 13.1 us: body(): call(final_kernel, 'final', (blocks(OWN, SLOTS), jax.ShapeDtypeStruct((N_...]
    gather x3 -> x0, local copies, waits for them, and re-layouts: 29.6 us -> none  [the longest x1 28.4 us: body(): jnp.take(blocks, index, axis=0)]
    concatenate x2 -> x0, other arithmetic: 28.2 us -> none  [padded(): value = jnp.concatenate([before, value, after], axis=dim)]
    unnamed x29 -> x8, local copies, waits for them, and re-layouts: 24.1 us -> 2.65 us
    ppermute x4 -> x8, starting transfers between devices: 9.06 us -> 26.3 us  [the longest x1 6.26 us: body(): far_ahead = lax.ppermute(far_m, AXES, from_direction(2))]
  transfers between devices with their start and end apart: 4 -> 8, of which waited for: 3 -> 4; matrix products, arithmetic and copies ran while one was open for 8% -> 0% of each run, Pallas kernels for 0% -> 22%
where the time goes in v1:
time: 102 us
  Pallas kernels  41.5 us (41%)
  starting transfers between devices  26.3 us (26%)
  blocking collectives  17.2 us (17%)
  waiting for transfers between devices  12.8 us (13%)
  local copies, waits for them, and re-layouts  3.31 us (3%)
    all_to_all x1, blocking collectives, body(): lines = lax.all_to_all(line, AXES, 0, 0, tiled=True)  17.2 us
    pallas_call x1, Pallas kernels, body(): call(final_kernel, 'final', (blocks(OWN, SLOTS), jax.ShapeDtypeStruct((N_...  13.1 us
    pallas_call x1, Pallas kernels, body(): call(local_kernel, 'local', (table, wides(OWN * SLOTS), blocks(OWN * SLOT...  12.9 us
    ppermute x1, starting transfers between devices, body(): far_ahead = lax.ppermute(far_m, AXES, from_direction(2))  6.26 us
    pallas_call x1, Pallas kernels, body(): call(pair_kernel, 'pair', (wides(16), wides(N_PAIR), blocks(OWN * SLOTS),...  6.21 us
    ppermute x1, waiting for transfers between devices, body(): late_behind = lax.ppermute(late_p, AXES, from_direction(3))  5.15 us
    ppermute x1, starting transfers between devices, body(): late_ahead = lax.ppermute(late_m, AXES, from_direction(4))  5.09 us
    pallas_call x1, Pallas kernels, body(): call(first_kernel, 'first', (blocks(OWN * SLOTS), table, blocks(10), bloc...  5.08 us
  transfers between devices with their start and end apart: 8, of which 4 were waited for; matrix products, arithmetic and copies ran while one was open for 0% of the time, Pallas kernels for 22%

profile of v1, /device:TPU:1, one launch (start us, length us, event | category | flops | bytes accessed | tf_op | source)
XLA Modules:
  0.0 101.9 jit_solution(11755845954537716489)
XLA Ops:
  0.6 0.0 copy-start.2
  0.6 0.7 copy-done.2
  1.4 0.0 copy-start.3
  1.4 5.1 %first.1 = (f32[48,128,128]{2,1,0:T(8,128)}, s32[344]{0:T(512)S(1)}, f32[10,128,128]{2,1,0:T(8,128)}, f32[10,128,128]{2,1,0:T(8,128)}, f32[8,128,128]{2,1,0:T(8,...) custom-call(s32[12,512]{1,0:T(8,128)S(1)} %bitcast.5, f32[48,128,128]{2,1,0:T(8,128)} %bitcast.8), custom_call_target="tpu_custom_call" | custom-call | bytes 10485760 | tf_op jit(solution)/shard_map/first/pallas_call | solution.py:454
  6.5 2.8 %collective-permute-start.4 = (f32[12,128,128]{2,1,0:T(8,128)}, f32[12,128,128]{2,1,0:T(8,128)S(1)}, u32[]{:S(2)}, u32[]{:S(2)}) collective-permute-start(f32[12,128,128]{2,1,0:T(8,128)} %get-tuple-element.34), channel_id=1, source_target_pairs={{120,0},{121,1},{122,2},{123,3},{124,4},{125,5},{126,6},{127,7},{1... | collective-permute-start | bytes 2359304 | tf_op jit(solution)/shard_map/ppermute | solution.py:464
  9.2 3.7 %collective-permute-start = (f32[10,128,128]{2,1,0:T(8,128)}, f32[10,128,128]{2,1,0:T(8,128)S(1)}, u32[]{:S(2)}, u32[]{:S(2)}) collective-permute-start(f32[10,128,128]{2,1,0:T(8,128)} %get-tuple-element.30), channel_id=1, source_target_pairs={{15,0},{8,1},{9,2},{10,3},{11,4},{12,5},{13,6},{14,7},{7,8},{0,9},... | collective-permute-start | bytes 1966088 | tf_op jit(solution)/shard_map/ppermute | solution.py:461
  13.0 4.3 %collective-permute-start.1 = (f32[10,128,128]{2,1,0:T(8,128)}, f32[10,128,128]{2,1,0:T(8,128)S(1)}, u32[]{:S(2)}, u32[]{:S(2)}) collective-permute-start(f32[10,128,128]{2,1,0:T(8,128)} %get-tuple-element.31), channel_id=1, source_target_pairs={{9,0},{10,1},{11,2},{12,3},{13,4},{14,5},{15,6},{8,7},{1,8},{2,9},... | collective-permute-start | bytes 1966088 | tf_op jit(solution)/shard_map/ppermute | solution.py:460
  17.3 0.0 collective-permute-start.2
  17.3 6.3 %collective-permute-start.3 = (f32[8,128,128]{2,1,0:T(8,128)S(1)}, f32[8,128,128]{2,1,0:T(8,128)S(1)}, u32[]{:S(2)}, u32[]{:S(2)}) collective-permute-start(f32[8,128,128]{2,1,0:T(8,128)S(1)} %get-tuple-element.33), channel_id=1, source_target_pairs={{121,0},{122,1},{123,2},{124,3},{125,4},{126,5},{127,6},{120,7},{1... | collective-permute-start | bytes 1572872 | tf_op jit(solution)/shard_map/ppermute | solution.py:462
  23.5 0.0 copy-done.3
  23.5 0.0 copy-start
  23.5 1.9 %copy-done = f32[48,128,128]{2,1,0:T(8,128)S(1)} copy-done((f32[48,128,128]{2,1,0:T(8,128)S(1)}, f32[48,128,128]{2,1,0:T(8,128)}, u32[]{:S(2)}) %copy-start) | copy-done | bytes 3145752
  25.4 12.9 %local.1 = (s32[344]{0:T(512)S(1)}, bf16[48,128,256]{2,1,0:T(8,128)(2,1)S(1)}, f32[48,128,128]{2,1,0:T(8,128)S(1)}, bf16[9,4,12,128,128]{4,3,2,1,0:T(8,128)(2,1)}) custom-call(s32[12,512]{1,0:T(8,128)S(1)} %bitcast.6, f32[48,128,128]{2,1,0:T(8,128)S(1)} %copy-done, s32[344]{0:T(512)S(1)} %get-tuple-element.26.tab_in, bf16[9,4,12,128,128]{4,3,2,1,0:T(8,128)(2,1)} %ham.1), custom_call_target="tpu_custom_call" | custom-call | flops 3221225472 | bytes 37748736 | tf_op jit(solution)/shard_map/local/pallas_call | solution.py:465
  38.3 3.8 %collective-permute-done.2.refs_0_.far_m = f32[8,128,128]{2,1,0:T(8,128)S(1)} collective-permute-done((f32[8,128,128]{2,1,0:T(8,128)}, f32[8,128,128]{2,1,0:T(8,128)S(1)}, u32[]{:S(2)}, u32[]{:S(2)}) %collective-permute-start.2) | collective-permute-done | bytes 524320 | tf_op jit(solution)/shard_map/ppermute | solution.py:463
  42.1 3.2 %collective-permute-done.3.refs_1_.far_p = f32[8,128,128]{2,1,0:T(8,128)S(1)} collective-permute-done((f32[8,128,128]{2,1,0:T(8,128)S(1)}, f32[8,128,128]{2,1,0:T(8,128)S(1)}, u32[]{:S(2)}, u32[]{:S(2)}) %collective-permute-start.3) | collective-permute-done | bytes 524320 | tf_op jit(solution)/shard_map/ppermute | solution.py:462
  45.4 0.6 collective-permute-done.behind.near_m
  46.0 0.0 collective-permute-done.1.ahead.near_p
  46.0 0.0 collective-permute-done.4.refs_2_.beside
  46.0 0.0 copy-done.1
  46.0 0.7 second.1
  46.7 4.1 %collective-permute-start.5 = (f32[16,128,128]{2,1,0:T(8,128)S(1)}, f32[16,128,128]{2,1,0:T(8,128)S(1)}, u32[]{:S(2)}, u32[]{:S(2)}) collective-permute-start(f32[16,128,128]{2,1,0:T(8,128)S(1)} %get-tuple-element.35.after), channel_id=1, source_target_pairs={{8,0},{9,1},{10,2},{11,3},{12,4},{13,5},{14,6},{15,7},{0,8},{1,9},... | collective-permute-start | bytes 3145736 | tf_op jit(solution)/shard_map/ppermute | solution.py:477
  50.8 0.0 collective-permute-start.6
  50.8 5.1 %collective-permute-start.7 = (f32[10,128,128]{2,1,0:T(8,128)S(1)}, f32[10,128,128]{2,1,0:T(8,128)S(1)}, u32[]{:S(2)}, u32[]{:S(2)}) collective-permute-start(f32[10,128,128]{2,1,0:T(8,128)S(1)} %get-tuple-element.36.also), channel_id=1, source_target_pairs={{1,0},{2,1},{3,2},{4,3},{5,4},{6,5},{7,6},{0,7},{9,8},{10,9},{11,1... | collective-permute-start | bytes 1966088 | tf_op jit(solution)/shard_map/ppermute | solution.py:475
  55.9 3.4 %early.1 = (bf16[16,128,256]{2,1,0:T(8,128)(2,1)S(1)}, bf16[34,128,256]{2,1,0:T(8,128)(2,1)S(1)}, f32[48,128,128]{2,1,0:T(8,128)S(1)}) custom-call(s32[344]{0:T(512)S(1)} %get-tuple-element.27.tab, bf16[48,128,256]{2,1,0:T(8,128)(2,1)S(1)} %get-tuple-element.28.wide, f32[48,128,128]{2,1,0:T(8,128)S(1)} %get-tuple-element.29.refs_3_.square_in, ...), custom_call_target="tpu_custom_call" | custom-call | flops 1476395008 | bytes 10485760 | tf_op jit(solution)/shard_map/early/pallas_call | solution.py:478
  59.4 0.0 collective-permute-done.5.pair_in
  59.4 6.2 %pair.1 = (bf16[16,128,256]{2,1,0:T(8,128)(2,1)S(1)}, bf16[10,128,256]{2,1,0:T(8,128)(2,1)S(1)}, f32[48,128,128]{2,1,0:T(8,128)S(1)}, f32[48,128,128]{2,1,0:T(8,128)S(1)}) custom-call(s32[344]{0:T(512)S(1)} %get-tuple-element.27.tab, bf16[48,128,256]{2,1,0:T(8,128)(2,1)S(1)} %get-tuple-element.28.wide, f32[48,128,128]{2,1,0:T(8,128)S(1)} %get-tuple-element.38.square_in, ...), custom_call_target="tpu_custom_call" | custom-call | flops 3758096384 | bytes 10485760 | tf_op jit(solution)/shard_map/pair/pallas_call | solution.py:484
  65.6 5.2 %collective-permute-done.6.behind = f32[10,128,128]{2,1,0:T(8,128)S(1)} collective-permute-done((f32[10,128,128]{2,1,0:T(8,128)S(1)}, f32[10,128,128]{2,1,0:T(8,128)S(1)}, u32[]{:S(2)}, u32[]{:S(2)}) %collective-permute-start.6) | collective-permute-done | bytes 655392 | tf_op jit(solution)/shard_map/ppermute | solution.py:476
  70.8 0.0 collective-permute-done.7.ahead
  70.8 13.1 %final.1 = (f32[4,12,128,128]{3,2,1,0:T(8,128)}, f32[128,128]{1,0:T(8,128)S(1)}) custom-call(s32[344]{0:T(512)S(1)} %get-tuple-element.27.tab, bf16[48,128,256]{2,1,0:T(8,128)(2,1)S(1)} %get-tuple-element.28.wide, bf16[16,128,256]{2,1,0:T(8,128)(2,1)S(1)} %get-tuple-element.37.own_early, bf16[16,128,256]{2,1,0:T(8,128)(2,1)S(1)} %get-tuple-element.39.own_late, ...), custom_call_target="tpu_custom_call" | custom-call | flops 3355443200 | bytes 31457280 | tf_op jit(solution)/shard_map/final/pallas_call | solution.py:490
  83.9 17.2 %all_to_all.9 = f32[128,1,128]{2,1,0:T(1,128)S(1)} all-to-all(f32[128,1,128]{2,1,0:T(1,128)S(1)} %bitcast.7), channel_id=1, replica_groups=mesh['row'=16,'col'=8] {'row','col'}, dimensions={0} | all-to-all | bytes 131072 | tf_op jit(solution)/shard_map/all_to_all | solution.py:501
  101.1 0.2 reduce_sum.9
  101.3 0.7 mul.8
  (2 shorter events, 0.0 us)
Async XLA Ops:
  0.6 0.8 copy-start.2
  1.4 22.1 %copy-start.3 = (s32[512,12]{0,1:T(8,128)S(1)}, s32[512,12]{0,1:T(8,128)}, u32[]{:S(2)}) copy-start(s32[512,12]{0,1:T(8,128)} %param.4) | copy-start | bytes 73732
  6.5 39.5 %collective-permute-start.4 = (f32[12,128,128]{2,1,0:T(8,128)}, f32[12,128,128]{2,1,0:T(8,128)S(1)}, u32[]{:S(2)}, u32[]{:S(2)}) collective-permute-start(f32[12,128,128]{2,1,0:T(8,128)} %get-tuple-element.34), channel_id=1, source_target_pairs={{120,0},{121,1},{122,2},{123,3},{124,4},{125,5},{126,6},{127,7},{1... | collective-permute-start | bytes 2359304 | tf_op jit(solution)/shard_map/ppermute | solution.py:464
  9.2 36.7 %collective-permute-start = (f32[10,128,128]{2,1,0:T(8,128)}, f32[10,128,128]{2,1,0:T(8,128)S(1)}, u32[]{:S(2)}, u32[]{:S(2)}) collective-permute-start(f32[10,128,128]{2,1,0:T(8,128)} %get-tuple-element.30), channel_id=1, source_target_pairs={{15,0},{8,1},{9,2},{10,3},{11,4},{12,5},{13,6},{14,7},{7,8},{0,9},... | collective-permute-start | bytes 1966088 | tf_op jit(solution)/shard_map/ppermute | solution.py:461
  13.0 33.0 %collective-permute-start.1 = (f32[10,128,128]{2,1,0:T(8,128)}, f32[10,128,128]{2,1,0:T(8,128)S(1)}, u32[]{:S(2)}, u32[]{:S(2)}) collective-permute-start(f32[10,128,128]{2,1,0:T(8,128)} %get-tuple-element.31), channel_id=1, source_target_pairs={{9,0},{10,1},{11,2},{12,3},{13,4},{14,5},{15,6},{8,7},{1,8},{2,9},... | collective-permute-start | bytes 1966088 | tf_op jit(solution)/shard_map/ppermute | solution.py:460
  17.3 24.9 %collective-permute-start.2 = (f32[8,128,128]{2,1,0:T(8,128)}, f32[8,128,128]{2,1,0:T(8,128)S(1)}, u32[]{:S(2)}, u32[]{:S(2)}) collective-permute-start(f32[8,128,128]{2,1,0:T(8,128)} %get-tuple-element.32), channel_id=1, source_target_pairs={{127,0},{120,1},{121,2},{122,3},{123,4},{124,5},{125,6},{126,7},{2... | collective-permute-start | bytes 1572872 | tf_op jit(solution)/shard_map/ppermute | solution.py:463
  17.3 28.1 %collective-permute-start.3 = (f32[8,128,128]{2,1,0:T(8,128)S(1)}, f32[8,128,128]{2,1,0:T(8,128)S(1)}, u32[]{:S(2)}, u32[]{:S(2)}) collective-permute-start(f32[8,128,128]{2,1,0:T(8,128)S(1)} %get-tuple-element.33), channel_id=1, source_target_pairs={{121,0},{122,1},{123,2},{124,3},{125,4},{126,5},{127,6},{120,7},{1... | collective-permute-start | bytes 1572872 | tf_op jit(solution)/shard_map/ppermute | solution.py:462
  23.5 1.9 %copy-start = (f32[48,128,128]{2,1,0:T(8,128)S(1)}, f32[48,128,128]{2,1,0:T(8,128)}, u32[]{:S(2)}) copy-start(f32[48,128,128]{2,1,0:T(8,128)} %get-tuple-element.25.dens) | copy-start | bytes 9437188
  25.4 20.6 %copy-start.1 = (f32[48,128,128]{2,1,0:T(8,128)S(1)}, f32[48,128,128]{2,1,0:T(8,128)}, u32[]{:S(2)}) copy-start(f32[48,128,128]{2,1,0:T(8,128)} %get-tuple-element.25.dens) | copy-start | bytes 9437188
  46.7 12.7 %collective-permute-start.5 = (f32[16,128,128]{2,1,0:T(8,128)S(1)}, f32[16,128,128]{2,1,0:T(8,128)S(1)}, u32[]{:S(2)}, u32[]{:S(2)}) collective-permute-start(f32[16,128,128]{2,1,0:T(8,128)S(1)} %get-tuple-element.35.after), channel_id=1, source_target_pairs={{8,0},{9,1},{10,2},{11,3},{12,4},{13,5},{14,6},{15,7},{0,8},{1,9},... | collective-permute-start | bytes 3145736 | tf_op jit(solution)/shard_map/ppermute | solution.py:477
  50.8 19.9 %collective-permute-start.6 = (f32[10,128,128]{2,1,0:T(8,128)S(1)}, f32[10,128,128]{2,1,0:T(8,128)S(1)}, u32[]{:S(2)}, u32[]{:S(2)}) collective-permute-start(f32[10,128,128]{2,1,0:T(8,128)S(1)} %get-tuple-element.44), channel_id=1, source_target_pairs={{7,0},{0,1},{1,2},{2,3},{3,4},{4,5},{5,6},{6,7},{15,8},{8,9},{9,10... | collective-permute-start | bytes 1966088 | tf_op jit(solution)/shard_map/ppermute | solution.py:476
  50.8 19.9 %collective-permute-start.7 = (f32[10,128,128]{2,1,0:T(8,128)S(1)}, f32[10,128,128]{2,1,0:T(8,128)S(1)}, u32[]{:S(2)}, u32[]{:S(2)}) collective-permute-start(f32[10,128,128]{2,1,0:T(8,128)S(1)} %get-tuple-element.36.also), channel_id=1, source_target_pairs={{1,0},{2,1},{3,2},{4,3},{5,4},{6,5},{7,6},{0,7},{9,8},{10,9},{11,1... | collective-permute-start | bytes 1966088 | tf_op jit(solution)/shard_map/ppermute | solution.py:475

commit v2 on v1

--- a/solution.py
+++ b/solution.py
@@ -108,14 +108,13 @@
     return [tab[at]] + [tab[at + m] for m in range(2, COUNT[f])]
 
 
-def fill(out, tab, dens, f):
-    for k in range(2):
-        out[k] = dens[own_of(tab, f, k)]
-        for m, n in enumerate(rest_of(tab, f, k)):
-            out[2 + k * (COUNT[f] - 1) + m] = dens[n]
-
-
-def first_kernel(pat_in, dens_in, dens, tab, near_m, near_p, far_m, far_p, beside, pat, sem):
+def fill(out, tab, dens, f, low=0, high=12):
+    numbers = [own_of(tab, f, k) for k in range(2)] + rest_of(tab, f, 0) + rest_of(tab, f, 1)
+    for i, n in enumerate(numbers[low:high]):
+        out[i] = dens[n]
+
+
+def first_kernel(pat_in, dens_in, tab, near_m, near_p, far_m, far_p, beside, dens, pat, sem):
     load = pltpu.make_async_copy(dens_in, dens, sem.at[0])
     load.start()
     pat_load = pltpu.make_async_copy(pat_in, pat, sem.at[1])
@@ -130,20 +129,20 @@
         fill(out, tab, dens, f)
         for k in range(2):
             out[8 + k] = dens[own_of(tab, edge, k)]
-    for out, f in ((far_m, 0), (far_p, 2), (beside, 1)):
+    for out, f in ((far_m, 0), (far_p, 2)):
         fill(out, tab, dens, f)
+    fill(beside, tab, dens, 1, 0, 2)
 
 
 def second_kernel(tab, dens, behind, ahead, *refs):
-    pair, late_m, late_p = refs[4:]
-    fill(pair, tab, dens, 6)
+    late_m, late_p, beside, pair_low, pair_high = refs[1:]
+    fill(pair_low, tab, dens, 6, 0, 8)
+    fill(pair_high, tab, dens, 6, 8, 12)
     for k in range(2):
-        pair[12 + k] = behind[8 + k]
-        pair[14 + k] = ahead[8 + k]
-    for f, out in ((3, late_m), (4, late_p)):
-        for k in range(2):
-            for m, n in enumerate(rest_of(tab, f, k)):
-                out[5 * k + m] = dens[n]
+        pair_high[4 + k] = behind[8 + k]
+        pair_high[6 + k] = ahead[8 + k]
+    for f, out in ((3, late_m), (4, late_p), (1, beside)):
+        fill(out, tab, dens, f, 2, 12)
 
 
 def far_table(pat, row, col, tab):
@@ -181,9 +180,8 @@
     return jnp.where(tab[T_NAME + g * SLOTS + 4 + d] == tab[T_LOW + d], 0, 1)
 
 
-def local_kernel(pat, dens, tab_in, ham, tab, wide, square, ham_out, zeros, sem):
-    for c in range(9):
-        pltpu.make_async_copy(ham.at[c], ham_out.at[c], sem.at[c]).start()
+def local_kernel(pat, dens, tab_in, after, tab, wide, square, zeros):
+    del after
     row = lax.axis_index("row")
     col = lax.axis_index("col")
     for i in range(T_LOW):
@@ -211,8 +209,6 @@
         return 0
 
     lax.fori_loop(0, OWN, rows, 0)
-    for c in range(9):
-        pltpu.make_async_copy(ham.at[c], ham_out.at[c], sem.at[c]).wait()
 
 
 def masked(match, left, zeros):
@@ -261,9 +257,9 @@
     return out, total
 
 
-EARLY = (0, 1, 2, 5, 7)
+EARLY = (0, 2, 5, 7)
 PAIR = (6,)
-LATE = (3, 4)
+LATE = (3, 4, 1)
 EARLY_AT, N_EARLY = offsets(EARLY)
 PAIR_AT, N_PAIR = offsets(PAIR)
 LATE_AT, N_LATE = offsets(LATE)
@@ -283,11 +279,11 @@
     return total
 
 
-def early_kernel(tab, wide, square_in, near_m, near_p, far_m, far_p, beside, after, also,
+def early_kernel(tab, wide, square_in, near_m, near_p, far_m, far_p, after, also,
                  own, early, square, back_buf, zeros):
     del after, also
     zeros[...] = jnp.zeros_like(zeros)
-    for d, ref in ((0, far_m), (1, beside), (2, far_p), (5, near_m), (7, near_p)):
+    for d, ref in ((0, far_m), (2, far_p), (5, near_m), (7, near_p)):
         for k in range(2):
             own[2 * d + k] = split(ref[k])
         widen(ref, 2, early, EARLY_AT[d], 2 * (COUNT[d] - 1))
@@ -310,12 +306,14 @@
     lax.fori_loop(0, OWN, rows, 0)
 
 
-def pair_kernel(tab, wide, square_in, pair_in, own, pair, square, cube, back_buf, wsq, zeros):
+def pair_kernel(tab, wide, square_in, low, high, beside,
+                own, pair, square, cube, back_buf, wsq, zeros):
     zeros[...] = jnp.zeros_like(zeros)
-    for d, start in ((6, 0), (3, 12), (4, 14)):
+    for d, ref, start in ((6, low, 0), (1, beside, 0), (3, high, 4), (4, high, 6)):
         for k in range(2):
-            own[2 * d + k] = split(pair_in[start + k])
-    widen(pair_in, 2, pair, 0, N_PAIR)
+            own[2 * d + k] = split(ref[start + k])
+    widen(low, 2, pair, 0, 6)
+    widen(high, 0, pair, 6, 4)
 
     def rows(g, _):
         back = own_terms(tab, g, PAIR + LATE)
@@ -345,23 +343,30 @@
     lax.fori_loop(0, OWN, rows, 0)
 
 
-def final_kernel(tab, wide, own_early, own_late, early, pair, square, cube, behind, ahead, ham,
-                 purified, virial, late, far_square, wsq, own_cube, out_buf, sums, zeros, out_sem):
+def final_kernel(tab, wide, own_early, own_late, early, pair, square, cube, behind, ahead, beside, ham,
+                 purified, virial, late, far_square, wsq, own_cube, back_buf, out_buf, sums, zeros, out_sem):
     zeros[...] = jnp.zeros_like(zeros)
     sums[...] = jnp.zeros_like(sums)
-    for d, ref in ((3, behind), (4, ahead)):
+    for d, ref in ((3, behind), (4, ahead), (1, beside)):
         widen(ref, 0, late, LATE_AT[d], 10)
 
+    def squares(g, _):
+        terms = far_terms(tab, g, LATE, LATE_AT, no_terms())
+        lefts = lambda left: wide[g * SLOTS + left]
+        sums_of = [halves(chain(None, terms[o], lefts, late, zeros)) for o in range(OWN, SLOTS)]
+        for i, total in enumerate(sums_of):
+            value = square[g * SLOTS + OWN + i] + total
+            far_square[g * 8 + i] = value
+            wsq[g * 8 + i] = split(value)
+        return 0
+
+    lax.fori_loop(0, OWN, squares, 0, unroll=4)
+
     def rows(g, _):
+        terms = far_terms(tab, g, PAIR, PAIR_AT, no_terms())
+        early_terms = far_terms(tab, g, EARLY, EARLY_AT, no_terms())
         late_terms = far_terms(tab, g, LATE, LATE_AT, no_terms())
-        pair_terms = far_terms(tab, g, PAIR, PAIR_AT, no_terms())
-        early_terms = far_terms(tab, g, EARLY, EARLY_AT, no_terms())
-        lefts = lambda left: wide[g * SLOTS + left]
-        for o in range(OWN, SLOTS):
-            total = chain(None, late_terms[o], lefts, late, zeros)
-            value = square[g * SLOTS + o] + halves(total)
-            far_square[o - OWN] = value
-            wsq[o - OWN] = split(value)
+        lefts = lambda left: wsq[g * 8 + left - OWN]
 
         def finish(o, value):
             slot = tab[T_SLOT + g * SLOTS + o]
@@ -370,24 +375,34 @@
                 part = ham[c, g, slot].astype(jnp.float32) * value
                 sums[c] += jnp.sum(part.reshape(EDGE // 8, 8, EDGE), axis=0)
 
-        lefts = lambda left: wsq[left - OWN]
-        for o in range(OWN):
-            own_cube[o] = cube[g * SLOTS + o]
-        for dirs, own in ((EARLY, own_early), (PAIR + LATE, own_late)):
-            for left, number, index in own_terms(tab, g, dirs):
-                term = halves(product(lefts(left), own[index]))
-                own_cube[number] = own_cube[number] + term
+        back = own_terms(tab, g, EARLY) + own_terms(tab, g, PAIR + LATE)
+        backs = []
+        for i, (left, number, index) in enumerate(back):
+            own = own_early if i < len(EARLY) else own_late
+            backs.append(halves(product(lefts(left), own[index])))
+        cubes = []
         for o in range(OWN, SLOTS):
-            total = chain(None, pair_terms[o], lefts, pair, zeros)
+            if len(cubes) == 0:
+                for i, total in enumerate(backs):
+                    back_buf[i] = total
+            total = chain(None, terms[o], lefts, pair, zeros)
             total = chain(total, early_terms[o], lefts, early, zeros)
             total = chain(total, late_terms[o], lefts, late, zeros)
-            finish(o, 3.0 * far_square[o - OWN] - 2.0 * (cube[g * SLOTS + o] + halves(total)))
+            cubes.append(halves(total))
+        for i, total in enumerate(cubes):
+            o = OWN + i
+            value = cube[g * SLOTS + o] + total
+            finish(o, 3.0 * far_square[g * 8 + i] - 2.0 * value)
         for o in range(OWN):
-            finish(o, 3.0 * square[g * SLOTS + o] - 2.0 * own_cube[o])
+            own_cube[o] = 3.0 * square[g * SLOTS + o] - 2.0 * cube[g * SLOTS + o]
+        for i, (left, number, index) in enumerate(back):
+            own_cube[number] = own_cube[number] - 2.0 * back_buf[i]
+        for o in range(OWN):
+            finish(o, own_cube[o])
         pltpu.make_async_copy(out_buf.at[g], purified.at[g], out_sem.at[g]).start()
         return 0
 
-    lax.fori_loop(0, OWN, rows, 0)
+    lax.fori_loop(0, OWN, rows, 0, unroll=2)
     lane = lax.broadcasted_iota(jnp.int32, (8, EDGE), 1)
     line = jnp.zeros((8, EDGE), jnp.float32)
     for c in range(9):
@@ -417,7 +432,7 @@
 BF16 = jnp.bfloat16
 
 
-def call(kernel, name, out, in_specs, out_specs, scratch, flops, moved, vmem=32):
+def call(kernel, name, out, in_specs, out_specs, scratch, flops, moved, vmem=12):
     return pl.pallas_call(
         kernel,
         out_shape=out,
@@ -451,51 +466,53 @@
 def body(density, pattern, ham_strain):
     dma = pltpu.SemaphoreType.DMA
     table = jax.ShapeDtypeStruct((T_SIZE,), jnp.int32)
-    dens, tab, near_m, near_p, far_m, far_p, beside = call(
-        first_kernel, "first",
-        (blocks(OWN * SLOTS), table, blocks(10), blocks(10), blocks(8), blocks(8), blocks(12)),
-        [HBM, HBM], (VMEM, SMEM) + (VMEM,) * 5,
-        [pltpu.SMEM((SLOTS, N_DEV * OWN), jnp.int32), dma((2,))], 0, 10, 53,
-    )(pattern.T, density.reshape(OWN * SLOTS, EDGE, EDGE))
+    dens = density.reshape(OWN * SLOTS, EDGE, EDGE)
+    tab, near_m, near_p, far_m, far_p, beside_own = call(
+        first_kernel, "first", (table, blocks(10), blocks(10), blocks(8), blocks(8), blocks(2)),
+        [HBM, HBM], (SMEM,) + (VMEM,) * 5,
+        [scratch(OWN * SLOTS), pltpu.SMEM((SLOTS, N_DEV * OWN), jnp.int32), dma((2,))], 0, 10, 56,
+    )(pattern.T, dens)
     near_ahead = lax.ppermute(near_m, AXES, from_direction(7))
     near_behind = lax.ppermute(near_p, AXES, from_direction(5))
     far_ahead = lax.ppermute(far_m, AXES, from_direction(2))
     far_behind = lax.ppermute(far_p, AXES, from_direction(0))
-    beside = lax.ppermute(beside, AXES, from_direction(1))
-    tab, wide, square, ham = call(
+    beside_own = lax.ppermute(beside_own, AXES, from_direction(1))
+    tab, wide, square = call(
         local_kernel, "local",
-        (table, wides(OWN * SLOTS), blocks(OWN * SLOTS),
-         jax.ShapeDtypeStruct(ham_strain.shape, BF16)),
-        [SMEM, VMEM, SMEM, HBM], (SMEM, VMEM, VMEM, VMEM), [wide_scratch(), dma((9,))], 192, 36,
-    )(pattern.T, dens, tab, ham_strain)
-    pair, late_m, late_p = call(
-        second_kernel, "second", (blocks(16), blocks(10), blocks(10)),
-        [SMEM] + [VMEM] * 3 + [ANY] * 4, (VMEM,) * 3, [], 0, 4,
-    )(tab, dens, near_behind, near_ahead, far_behind, far_ahead, beside, square)
+        (table, wides(OWN * SLOTS), blocks(OWN * SLOTS)),
+        [SMEM, VMEM, SMEM, ANY], (SMEM,) + (VMEM,) * 2, [wide_scratch()], 400, 9,
+    )(pattern.T, dens, tab, beside_own)
+    late_m, late_p, beside, pair_low, pair_high = call(
+        second_kernel, "second", (blocks(10), blocks(10), blocks(10), blocks(8), blocks(8)),
+        [SMEM] + [VMEM] * 3 + [ANY], (VMEM,) * 5, [], 0, 5,
+    )(tab, dens, near_behind, near_ahead, square)
     late_ahead = lax.ppermute(late_m, AXES, from_direction(4))
     late_behind = lax.ppermute(late_p, AXES, from_direction(3))
-    pair_in = lax.ppermute(pair, AXES, from_direction(6))
+    pair_low_in = lax.ppermute(pair_low, AXES, from_direction(6))
+    pair_high_in = lax.ppermute(pair_high, AXES, from_direction(6))
+    beside_in = lax.ppermute(beside, AXES, from_direction(1))
     own_early, early, square = call(
         early_kernel, "early",
         (wides(16), wides(N_EARLY), blocks(OWN * SLOTS)),
-        [SMEM] + [VMEM] * 7 + [ANY] * 2, (VMEM,) * 3,
-        [scratch(8), wide_scratch()], 88, 10,
-    )(tab, wide, square, near_behind, near_ahead, far_behind, far_ahead, beside, pair, late_m)
+        [SMEM] + [VMEM] * 6 + [ANY] * 2, (VMEM,) * 3,
+        [scratch(8), wide_scratch()], 0, 0,
+    )(tab, wide, square, near_behind, near_ahead, far_behind, far_ahead, beside, late_m)
     own_late, pair, square, cube = call(
         pair_kernel, "pair",
         (wides(16), wides(N_PAIR), blocks(OWN * SLOTS), blocks(OWN * SLOTS)),
-        [SMEM] + [VMEM] * 3, (VMEM,) * 4,
-        [scratch(8), wide_scratch(OWN), wide_scratch()], 224, 10,
-    )(tab, wide, square, pair_in)
+        [SMEM] + [VMEM] * 5, (VMEM,) * 4,
+        [scratch(8), wide_scratch(OWN), wide_scratch()], 0, 0,
+    )(tab, wide, square, pair_low_in, pair_high_in, beside_own)
     purified, line = call(
         final_kernel, "final",
         (blocks(OWN, SLOTS), jax.ShapeDtypeStruct((N_DEV, EDGE), F32)),
-        [SMEM] + [VMEM] * 10, (ANY, VMEM),
+        [SMEM] + [VMEM] * 11, (ANY, VMEM),
         [
-            wide_scratch(N_LATE), scratch(8), wide_scratch(8), scratch(OWN),
+            wide_scratch(N_LATE), scratch(8 * OWN), wide_scratch(8 * OWN), scratch(OWN), scratch(8),
             scratch(OWN, SLOTS), pltpu.VMEM((9, 8, EDGE), F32), wide_scratch(), dma((OWN,)),
         ], 200, 30,
-    )(tab, wide, own_early, own_late, early, pair, square, cube, late_behind, late_ahead, ham)
+    )(tab, wide, own_early, own_late, early, pair, square, cube, late_behind, late_ahead, beside_in,
+      ham_strain)
     total_blocks = N_DEV * OWN
     factor = 1.0 / math.sqrt(float(total_blocks * SLOTS * EDGE * EDGE))
     lines = lax.all_to_all(line, AXES, 0, 0, tiled=True)

time: 102 us -> 92.5 us (0.907)
  Pallas kernels: 41.5 us -> 31.6 us
  blocking collectives: 17.2 us -> 21.8 us
  starting transfers between devices: 26.3 us -> 24.2 us
  local copies, waits for them, and re-layouts: 3.31 us -> 1.36 us
    ppermute x1, waiting for transfers between devices: 0.01 us -> 5.39 us  [body(): near_ahead = lax.ppermute(near_m, AXES, from_direction(7))]
    pallas_call x1, Pallas kernels: 12.9 us -> 8.15 us  [body(): call(local_kernel, 'local', (table, wides(OWN * SLOTS), blocks(OWN * SLOT...]
    all_to_all x1, blocking collectives: 17.2 us -> 21.8 us  [body(): lines = lax.all_to_all(line, AXES, 0, 0, tiled=True)]
    pallas_call x1, Pallas kernels: 13.1 us -> 9.16 us  [body(): call(final_kernel, 'final', (blocks(OWN, SLOTS), jax.ShapeDtypeStruct((N_...]
    ppermute x1, waiting for transfers between devices: 3.82 us -> 0.01 us  [body(): far_behind = lax.ppermute(far_p, AXES, from_direction(0))]
    ppermute x1, waiting for transfers between devices: 3.24 us -> 0.01 us  [body(): far_ahead = lax.ppermute(far_m, AXES, from_direction(2))]
    ppermute x1, waiting for transfers between devices: 0.58 us -> 3.58 us  [body(): near_behind = lax.ppermute(near_p, AXES, from_direction(5))]
    ppermute x2 -> x4, starting transfers between devices: 6.91 us -> 4.77 us  [the longest x1 2.77 us: body(): beside_own = lax.ppermute(beside_own, AXES, from_direction(1))]
  transfers between devices with their start and end apart: 8 -> 10, of which waited for: 4 -> 3; matrix products, arithmetic and copies ran while one was open for 0% -> 0% of each run, Pallas kernels for 22% -> 20%
where the time goes in v2:
time: 92.5 us; the launch traced here: 92.4 us
  Pallas kernels  31.6 us (34%)
  starting transfers between devices  24.2 us (26%)
  blocking collectives  21.8 us (24%)
  waiting for transfers between devices  12.4 us (13%)
  local copies, waits for them, and re-layouts  1.36 us (1%)
    all_to_all x1, blocking collectives, body(): lines = lax.all_to_all(line, AXES, 0, 0, tiled=True)  21.8 us
    pallas_call x1, Pallas kernels, body(): call(final_kernel, 'final', (blocks(OWN, SLOTS), jax.ShapeDtypeStruct((N_...  9.16 us
    pallas_call x1, Pallas kernels, body(): call(local_kernel, 'local', (table, wides(OWN * SLOTS), blocks(OWN * SLOT...  8.15 us
    pallas_call x1, Pallas kernels, body(): call(pair_kernel, 'pair', (wides(16), wides(N_PAIR), blocks(OWN * SLOTS),...  6.45 us
    ppermute x1, starting transfers between devices, body(): far_ahead = lax.ppermute(far_m, AXES, from_direction(2))  6.26 us
    ppermute x1, waiting for transfers between devices, body(): near_ahead = lax.ppermute(near_m, AXES, from_direction(7))  5.39 us
    ppermute x1, starting transfers between devices, body(): near_ahead = lax.ppermute(near_m, AXES, from_direction(7))  4.29 us
    pallas_call x1, Pallas kernels, body(): call(first_kernel, 'first', (table, blocks(10), blocks(10), blocks(8), bl...  4.26 us
  transfers between devices with their start and end apart: 10, of which 3 were waited for; matrix products, arithmetic and copies ran while one was open for 0% of the time, Pallas kernels for 20%

profile of v2, /device:TPU:1, one launch (start us, length us, event | category | flops | bytes accessed | tf_op | source)
XLA Modules:
  0.0 92.4 jit_solution(11816880780782386995)
XLA Ops:
  0.6 4.3 %first.1 = (s32[344]{0:T(512)}, f32[10,128,128]{2,1,0:T(8,128)}, f32[10,128,128]{2,1,0:T(8,128)}, f32[8,128,128]{2,1,0:T(8,128)}, f32[8,128,128]{2,1,0:T(8,128)}, /*index=5*/f32[2,128,128]{2,1,0:T(8,128)}) custom-call(s32[12,512]{1,0:T(8,128)} %bitcast.11, f32[48,128,128]{2,1,0:T(8,128)} %bitcast.7), custom_call_target="tpu_custom_call" | custom-call | bytes 10485760 | tf_op jit(solution)/shard_map/first/pallas_call | solution.py:470
  4.9 2.8 %collective-permute-start = (f32[2,128,128]{2,1,0:T(8,128)}, f32[2,128,128]{2,1,0:T(8,128)S(1)}, u32[]{:S(2)}, u32[]{:S(2)}) collective-permute-start(f32[2,128,128]{2,1,0:T(8,128)} %get-tuple-element.26), channel_id=1, source_target_pairs={{120,0},{121,1},{122,2},{123,3},{124,4},{125,5},{126,6},{127,7},{1... | collective-permute-start | bytes 393224 | tf_op jit(solution)/shard_map/ppermute | solution.py:479
  7.7 3.7 %collective-permute-start.1 = (f32[10,128,128]{2,1,0:T(8,128)}, f32[10,128,128]{2,1,0:T(8,128)S(1)}, u32[]{:S(2)}, u32[]{:S(2)}) collective-permute-start(f32[10,128,128]{2,1,0:T(8,128)} %get-tuple-element.30), channel_id=1, source_target_pairs={{15,0},{8,1},{9,2},{10,3},{11,4},{12,5},{13,6},{14,7},{7,8},{0,9},... | collective-permute-start | bytes 1966088 | tf_op jit(solution)/shard_map/ppermute | solution.py:476
  11.4 4.3 %collective-permute-start.2 = (f32[10,128,128]{2,1,0:T(8,128)}, f32[10,128,128]{2,1,0:T(8,128)S(1)}, u32[]{:S(2)}, u32[]{:S(2)}) collective-permute-start(f32[10,128,128]{2,1,0:T(8,128)} %get-tuple-element.31), channel_id=1, source_target_pairs={{9,0},{10,1},{11,2},{12,3},{13,4},{14,5},{15,6},{8,7},{1,8},{2,9},... | collective-permute-start | bytes 1966088 | tf_op jit(solution)/shard_map/ppermute | solution.py:475
  15.7 0.0 collective-permute-start.3
  15.7 6.3 %collective-permute-start.4 = (f32[8,128,128]{2,1,0:T(8,128)}, f32[8,128,128]{2,1,0:T(8,128)S(1)}, u32[]{:S(2)}, u32[]{:S(2)}) collective-permute-start(f32[8,128,128]{2,1,0:T(8,128)} %get-tuple-element.33), channel_id=1, source_target_pairs={{121,0},{122,1},{123,2},{124,3},{125,4},{126,5},{127,6},{120,7},{1... | collective-permute-start | bytes 1572872 | tf_op jit(solution)/shard_map/ppermute | solution.py:477
  22.0 0.0 collective-permute-done.after.beside
  22.0 0.0 copy-start.2
  22.0 0.7 copy-done.2
  22.7 8.2 %local.1 = (s32[344]{0:T(512)S(1)}, bf16[48,128,256]{2,1,0:T(8,128)(2,1)S(1)}, f32[48,128,128]{2,1,0:T(8,128)S(1)}) custom-call(s32[12,512]{1,0:T(8,128)S(1)} %bitcast.12, f32[48,128,128]{2,1,0:T(8,128)S(1)} %bitcast.8, s32[344]{0:T(512)S(1)} %copy-done.2, f32[2,128,128]{2,1,0:T(8,128)S(1)} %collective-permute-done.after.beside), custom_call_target="tpu_custom_call" | custom-call | flops 6710886400 | bytes 9437184 | tf_op jit(solution)/shard_map/local/pallas_call | solution.py:480
  30.8 3.6 %collective-permute-done.1.behind.near_m = f32[10,128,128]{2,1,0:T(8,128)S(1)} collective-permute-done((f32[10,128,128]{2,1,0:T(8,128)}, f32[10,128,128]{2,1,0:T(8,128)S(1)}, u32[]{:S(2)}, u32[]{:S(2)}) %collective-permute-start.1) | collective-permute-done | bytes 655392 | tf_op jit(solution)/shard_map/ppermute | solution.py:476
  34.4 5.4 %collective-permute-done.2.ahead.near_p = f32[10,128,128]{2,1,0:T(8,128)S(1)} collective-permute-done((f32[10,128,128]{2,1,0:T(8,128)}, f32[10,128,128]{2,1,0:T(8,128)S(1)}, u32[]{:S(2)}, u32[]{:S(2)}) %collective-permute-start.2) | collective-permute-done | bytes 655392 | tf_op jit(solution)/shard_map/ppermute | solution.py:475
  39.8 0.8 second.1
  40.5 1.4 %collective-permute-start.7 = (f32[10,128,128]{2,1,0:T(8,128)S(1)}, f32[10,128,128]{2,1,0:T(8,128)S(1)}, u32[]{:S(2)}, u32[]{:S(2)}) collective-permute-start(f32[10,128,128]{2,1,0:T(8,128)S(1)} %get-tuple-element.45), channel_id=1, source_target_pairs={{7,0},{0,1},{1,2},{2,3},{3,4},{4,5},{5,6},{6,7},{15,8},{8,9},{9,10... | collective-permute-start | bytes 1966088 | tf_op jit(solution)/shard_map/ppermute | solution.py:490
  42.0 0.0 collective-permute-start.9
  42.0 3.8 %collective-permute-start.8 = (f32[10,128,128]{2,1,0:T(8,128)S(1)}, f32[10,128,128]{2,1,0:T(8,128)S(1)}, u32[]{:S(2)}, u32[]{:S(2)}) collective-permute-start(f32[10,128,128]{2,1,0:T(8,128)S(1)} %get-tuple-element.35.also), channel_id=1, source_target_pairs={{1,0},{2,1},{3,2},{4,3},{5,4},{6,5},{7,6},{0,7},{9,8},{10,9},{11,1... | collective-permute-start | bytes 1966088 | tf_op jit(solution)/shard_map/ppermute | solution.py:489
  45.7 0.0 collective-permute-done.3.far_m
  45.7 1.7 %collective-permute-start.5 = (f32[8,128,128]{2,1,0:T(8,128)S(1)}, f32[8,128,128]{2,1,0:T(8,128)S(1)}, u32[]{:S(2)}, u32[]{:S(2)}) collective-permute-start(f32[8,128,128]{2,1,0:T(8,128)S(1)} %get-tuple-element.38), channel_id=1, source_target_pairs={{8,0},{9,1},{10,2},{11,3},{12,4},{13,5},{14,6},{15,7},{0,8},{1,9},... | collective-permute-start | bytes 1572872 | tf_op jit(solution)/shard_map/ppermute | solution.py:491
  47.5 0.0 collective-permute-done.4.far_p
  47.5 0.3 collective-permute-start.6
  47.7 2.9 %early.1 = (bf16[16,128,256]{2,1,0:T(8,128)(2,1)S(1)}, bf16[24,128,256]{2,1,0:T(8,128)(2,1)S(1)}, f32[48,128,128]{2,1,0:T(8,128)S(1)}) custom-call(s32[344]{0:T(512)S(1)} %get-tuple-element.27.tab, bf16[48,128,256]{2,1,0:T(8,128)(2,1)S(1)} %get-tuple-element.28.wide, f32[48,128,128]{2,1,0:T(8,128)S(1)} %get-tuple-element.29.refs_0_.square_in, ...), custom_call_target="tpu_custom_call" | custom-call | tf_op jit(solution)/shard_map/early/pallas_call | solution.py:494
  50.6 0.0 collective-permute-done.5.low
  50.6 0.0 collective-permute-done.6.high
  50.6 6.4 %pair.1 = (bf16[16,128,256]{2,1,0:T(8,128)(2,1)S(1)}, bf16[10,128,256]{2,1,0:T(8,128)(2,1)S(1)}, f32[48,128,128]{2,1,0:T(8,128)S(1)}, f32[48,128,128]{2,1,0:T(8,128)S(1)}) custom-call(s32[344]{0:T(512)S(1)} %get-tuple-element.27.tab, bf16[48,128,256]{2,1,0:T(8,128)(2,1)S(1)} %get-tuple-element.28.wide, f32[48,128,128]{2,1,0:T(8,128)S(1)} %get-tuple-element.37.square_in, ...), custom_call_target="tpu_custom_call" | custom-call | tf_op jit(solution)/shard_map/pair/pallas_call | solution.py:500
  57.1 3.5 %collective-permute-done.7.behind = f32[10,128,128]{2,1,0:T(8,128)S(1)} collective-permute-done((f32[10,128,128]{2,1,0:T(8,128)S(1)}, f32[10,128,128]{2,1,0:T(8,128)S(1)}, u32[]{:S(2)}, u32[]{:S(2)}) %collective-permute-start.7) | collective-permute-done | bytes 655392 | tf_op jit(solution)/shard_map/ppermute | solution.py:490
  60.5 0.0 collective-permute-done.9.beside
  60.5 0.0 collective-permute-done.8.ahead
  60.5 0.0 slice-done
  60.6 9.2 %final.1 = (f32[4,12,128,128]{3,2,1,0:T(8,128)}, f32[128,128]{1,0:T(8,128)S(1)}) custom-call(s32[344]{0:T(512)S(1)} %get-tuple-element.27.tab, bf16[48,128,256]{2,1,0:T(8,128)(2,1)S(1)} %get-tuple-element.28.wide, bf16[16,128,256]{2,1,0:T(8,128)(2,1)S(1)} %get-tuple-element.36.own_early, bf16[16,128,256]{2,1,0:T(8,128)(2,1)S(1)} %get-tuple-element.40.own_late, ...), custom_call_target="tpu_custom_call" | custom-call | flops 3355443200 | bytes 31457280 | tf_op jit(solution)/shard_map/final/pallas_call | solution.py:506
  69.7 21.8 %all_to_all.9 = f32[128,1,128]{2,1,0:T(1,128)S(1)} all-to-all(f32[128,1,128]{2,1,0:T(1,128)S(1)} %bitcast.10), channel_id=1, replica_groups=mesh['row'=16,'col'=8] {'row','col'}, dimensions={0} | all-to-all | bytes 131072 | tf_op jit(solution)/shard_map/all_to_all | solution.py:518
  91.5 0.2 reduce_sum.9
  91.7 0.7 mul.8
  (13 shorter events, 0.0 us)
Async XLA Ops:
  0.6 21.3 %copy-start.1 = (s32[512,12]{0,1:T(8,128)S(1)}, s32[512,12]{0,1:T(8,128)}, u32[]{:S(2)}) copy-start(s32[512,12]{0,1:T(8,128)} %param.4) | copy-start | bytes 73732
  0.6 21.3 %copy-start = (f32[4,12,128,128]{3,2,1,0:T(8,128)S(1)}, f32[4,12,128,128]{3,2,1,0:T(8,128)}, u32[]{:S(2)}) copy-start(f32[4,12,128,128]{3,2,1,0:T(8,128)} %param.3) | copy-start | bytes 9437188
  4.9 17.0 %collective-permute-start = (f32[2,128,128]{2,1,0:T(8,128)}, f32[2,128,128]{2,1,0:T(8,128)S(1)}, u32[]{:S(2)}, u32[]{:S(2)}) collective-permute-start(f32[2,128,128]{2,1,0:T(8,128)} %get-tuple-element.26), channel_id=1, source_target_pairs={{120,0},{121,1},{122,2},{123,3},{124,4},{125,5},{126,6},{127,7},{1... | collective-permute-start | bytes 393224 | tf_op jit(solution)/shard_map/ppermute | solution.py:479
  7.7 26.7 %collective-permute-start.1 = (f32[10,128,128]{2,1,0:T(8,128)}, f32[10,128,128]{2,1,0:T(8,128)S(1)}, u32[]{:S(2)}, u32[]{:S(2)}) collective-permute-start(f32[10,128,128]{2,1,0:T(8,128)} %get-tuple-element.30), channel_id=1, source_target_pairs={{15,0},{8,1},{9,2},{10,3},{11,4},{12,5},{13,6},{14,7},{7,8},{0,9},... | collective-permute-start | bytes 1966088 | tf_op jit(solution)/shard_map/ppermute | solution.py:476
  11.4 28.4 %collective-permute-start.2 = (f32[10,128,128]{2,1,0:T(8,128)}, f32[10,128,128]{2,1,0:T(8,128)S(1)}, u32[]{:S(2)}, u32[]{:S(2)}) collective-permute-start(f32[10,128,128]{2,1,0:T(8,128)} %get-tuple-element.31), channel_id=1, source_target_pairs={{9,0},{10,1},{11,2},{12,3},{13,4},{14,5},{15,6},{8,7},{1,8},{2,9},... | collective-permute-start | bytes 1966088 | tf_op jit(solution)/shard_map/ppermute | solution.py:475
  15.7 30.0 %collective-permute-start.3 = (f32[8,128,128]{2,1,0:T(8,128)}, f32[8,128,128]{2,1,0:T(8,128)S(1)}, u32[]{:S(2)}, u32[]{:S(2)}) collective-permute-start(f32[8,128,128]{2,1,0:T(8,128)} %get-tuple-element.32), channel_id=1, source_target_pairs={{127,0},{120,1},{121,2},{122,3},{123,4},{124,5},{125,6},{126,7},{2... | collective-permute-start | bytes 1572872 | tf_op jit(solution)/shard_map/ppermute | solution.py:478
  15.7 31.8 %collective-permute-start.4 = (f32[8,128,128]{2,1,0:T(8,128)}, f32[8,128,128]{2,1,0:T(8,128)S(1)}, u32[]{:S(2)}, u32[]{:S(2)}) collective-permute-start(f32[8,128,128]{2,1,0:T(8,128)} %get-tuple-element.33), channel_id=1, source_target_pairs={{121,0},{122,1},{123,2},{124,3},{125,4},{126,5},{127,6},{120,7},{1... | collective-permute-start | bytes 1572872 | tf_op jit(solution)/shard_map/ppermute | solution.py:477
  22.0 0.7 copy-start.2
  22.7 37.9 %slice-start = ((s8[14155776]{0:T(1024)(128)(4,1)}), s8[4194304]{0:T(1024)(128)(4,1)S(1)}, s32[]{:S(2)}) async-start(s8[14155776]{0:T(1024)(128)(4,1)} %bitcast.5), calls=%async_computation.1 | async-start | bytes 8388608
  22.7 37.9 %slice-start.1 = ((s8[14155776]{0:T(1024)(128)(4,1)}), s8[4194304]{0:T(1024)(128)(4,1)S(1)}, s32[]{:S(2)}) async-start(s8[14155776]{0:T(1024)(128)(4,1)} %bitcast.5), calls=%async_computation.2 | async-start | bytes 8388608
  39.8 20.8 %slice-start.2 = ((s8[14155776]{0:T(1024)(128)(4,1)}), s8[4194304]{0:T(1024)(128)(4,1)S(1)}, s32[]{:S(2)}) async-start(s8[14155776]{0:T(1024)(128)(4,1)} %bitcast.5), calls=%async_computation.3 | async-start | bytes 8388608
  40.5 20.0 %collective-permute-start.7 = (f32[10,128,128]{2,1,0:T(8,128)S(1)}, f32[10,128,128]{2,1,0:T(8,128)S(1)}, u32[]{:S(2)}, u32[]{:S(2)}) collective-permute-start(f32[10,128,128]{2,1,0:T(8,128)S(1)} %get-tuple-element.45), channel_id=1, source_target_pairs={{7,0},{0,1},{1,2},{2,3},{3,4},{4,5},{5,6},{6,7},{15,8},{8,9},{9,10... | collective-permute-start | bytes 1966088 | tf_op jit(solution)/shard_map/ppermute | solution.py:490
  42.0 18.6 %collective-permute-start.9 = (f32[10,128,128]{2,1,0:T(8,128)S(1)}, f32[10,128,128]{2,1,0:T(8,128)S(1)}, u32[]{:S(2)}, u32[]{:S(2)}) collective-permute-start(f32[10,128,128]{2,1,0:T(8,128)S(1)} %get-tuple-element.34.after), channel_id=1, source_target_pairs={{120,0},{121,1},{122,2},{123,3},{124,4},{125,5},{126,6},{127,7},{1... | collective-permute-start | bytes 1966088 | tf_op jit(solution)/shard_map/ppermute | solution.py:493
  42.0 18.6 %collective-permute-start.8 = (f32[10,128,128]{2,1,0:T(8,128)S(1)}, f32[10,128,128]{2,1,0:T(8,128)S(1)}, u32[]{:S(2)}, u32[]{:S(2)}) collective-permute-start(f32[10,128,128]{2,1,0:T(8,128)S(1)} %get-tuple-element.35.also), channel_id=1, source_target_pairs={{1,0},{2,1},{3,2},{4,3},{5,4},{6,5},{7,6},{0,7},{9,8},{10,9},{11,1... | collective-permute-start | bytes 1966088 | tf_op jit(solution)/shard_map/ppermute | solution.py:489
  45.7 4.9 %collective-permute-start.5 = (f32[8,128,128]{2,1,0:T(8,128)S(1)}, f32[8,128,128]{2,1,0:T(8,128)S(1)}, u32[]{:S(2)}, u32[]{:S(2)}) collective-permute-start(f32[8,128,128]{2,1,0:T(8,128)S(1)} %get-tuple-element.38), channel_id=1, source_target_pairs={{8,0},{9,1},{10,2},{11,3},{12,4},{13,5},{14,6},{15,7},{0,8},{1,9},... | collective-permute-start | bytes 1572872 | tf_op jit(solution)/shard_map/ppermute | solution.py:491
  47.5 3.2 %collective-permute-start.6 = (f32[8,128,128]{2,1,0:T(8,128)S(1)}, f32[8,128,128]{2,1,0:T(8,128)S(1)}, u32[]{:S(2)}, u32[]{:S(2)}) collective-permute-start(f32[8,128,128]{2,1,0:T(8,128)S(1)} %get-tuple-element.39), channel_id=1, source_target_pairs={{8,0},{9,1},{10,2},{11,3},{12,4},{13,5},{14,6},{15,7},{0,8},{1,9},... | collective-permute-start | bytes 1572872 | tf_op jit(solution)/shard_map/ppermute | solution.py:492
  47.7 12.8 %slice-start.3 = ((s8[14155776]{0:T(1024)(128)(4,1)}), s8[1572864]{0:T(1024)(128)(4,1)S(1)}, s32[]{:S(2)}) async-start(s8[14155776]{0:T(1024)(128)(4,1)} %bitcast.5), calls=%async_computation.4 | async-start | bytes 3145728

commit v3 on v2

--- a/solution.py
+++ b/solution.py
@@ -134,15 +134,18 @@
     fill(beside, tab, dens, 1, 0, 2)
 
 
+def late_kernel(tab, dens, *refs):
+    for f, out in zip((3, 4, 1), refs[1:]):
+        fill(out, tab, dens, f, 2, 12)
+
+
 def second_kernel(tab, dens, behind, ahead, *refs):
-    late_m, late_p, beside, pair_low, pair_high = refs[1:]
+    pair_low, pair_high = refs
     fill(pair_low, tab, dens, 6, 0, 8)
     fill(pair_high, tab, dens, 6, 8, 12)
     for k in range(2):
         pair_high[4 + k] = behind[8 + k]
         pair_high[6 + k] = ahead[8 + k]
-    for f, out in ((3, late_m), (4, late_p), (1, beside)):
-        fill(out, tab, dens, f, 2, 12)
 
 
 def far_table(pat, row, col, tab):
@@ -482,10 +485,14 @@
         (table, wides(OWN * SLOTS), blocks(OWN * SLOTS)),
         [SMEM, VMEM, SMEM, ANY], (SMEM,) + (VMEM,) * 2, [wide_scratch()], 400, 9,
     )(pattern.T, dens, tab, beside_own)
-    late_m, late_p, beside, pair_low, pair_high = call(
-        second_kernel, "second", (blocks(10), blocks(10), blocks(10), blocks(8), blocks(8)),
-        [SMEM] + [VMEM] * 3 + [ANY], (VMEM,) * 5, [], 0, 5,
-    )(tab, dens, near_behind, near_ahead, square)
+    late_m, late_p, beside = call(
+        late_kernel, "late", (blocks(10), blocks(10), blocks(10)),
+        [SMEM, VMEM, ANY], (VMEM,) * 3, [], 0, 3,
+    )(tab, dens, square)
+    pair_low, pair_high = call(
+        second_kernel, "second", (blocks(8), blocks(8)),
+        [SMEM] + [VMEM] * 3, (VMEM,) * 2, [], 0, 3,
+    )(tab, dens, near_behind, near_ahead)
     late_ahead = lax.ppermute(late_m, AXES, from_direction(4))
     late_behind = lax.ppermute(late_p, AXES, from_direction(3))
     pair_low_in = lax.ppermute(pair_low, AXES, from_direction(6))

time: 92.5 us -> 89.3 us (0.965)
  waiting for transfers between devices: 12.4 us -> 5.51 us
  starting transfers between devices: 24.2 us -> 26.5 us
    ppermute x1, waiting for transfers between devices: 3.45 us -> 0.01 us  [body(): late_behind = lax.ppermute(late_p, AXES, from_direction(3))]
    ppermute x1, waiting for transfers between devices: 5.39 us -> 2.14 us  [body(): near_ahead = lax.ppermute(near_m, AXES, from_direction(7))]
    ppermute x1, starting transfers between devices: 0.01 us -> 3.25 us  [body(): beside_in = lax.ppermute(beside, AXES, from_direction(1))]
    ppermute x1, starting transfers between devices: 1.74 us -> 3.87 us  [body(): pair_low_in = lax.ppermute(pair_low, AXES, from_direction(6))]
    ppermute x1, starting transfers between devices: 3.75 us -> 2.02 us  [body(): late_ahead = lax.ppermute(late_m, AXES, from_direction(4))]
    ppermute x1, starting transfers between devices: 1.41 us -> 0.08 us  [body(): late_behind = lax.ppermute(late_p, AXES, from_direction(3))]
  transfers between devices with their start and end apart: 10 -> 10, of which waited for: 3 -> 3; matrix products, arithmetic and copies ran while one was open for 0% -> 0% of each run, Pallas kernels for 20% -> 21%
where the time goes in v3:
time: 89.3 us; the launch traced here: 89.2 us
  Pallas kernels  32.2 us (36%)
  starting transfers between devices  26.5 us (30%)
  blocking collectives  22.7 us (25%)
  waiting for transfers between devices  5.51 us (6%)
  local copies, waits for them, and re-layouts  1.37 us (2%)
    all_to_all x1, blocking collectives, body(): lines = lax.all_to_all(line, AXES, 0, 0, tiled=True)  22.7 us
    pallas_call x1, Pallas kernels, body(): call(final_kernel, 'final', (blocks(OWN, SLOTS), jax.ShapeDtypeStruct((N_...  9.15 us
    pallas_call x1, Pallas kernels, body(): call(local_kernel, 'local', (table, wides(OWN * SLOTS), blocks(OWN * SLOT...  8.15 us
    pallas_call x1, Pallas kernels, body(): call(pair_kernel, 'pair', (wides(16), wides(N_PAIR), blocks(OWN * SLOTS),...  6.45 us
    ppermute x1, starting transfers between devices, body(): far_ahead = lax.ppermute(far_m, AXES, from_direction(2))  6.26 us
    ppermute x1, starting transfers between devices, body(): near_ahead = lax.ppermute(near_m, AXES, from_direction(7))  4.29 us
    pallas_call x1, Pallas kernels, body(): call(first_kernel, 'first', (table, blocks(10), blocks(10), blocks(8), bl...  4.25 us
    ppermute x1, starting transfers between devices, body(): pair_low_in = lax.ppermute(pair_low, AXES, from_direction(6))  3.87 us
  transfers between devices with their start and end apart: 10, of which 3 were waited for; matrix products, arithmetic and copies ran while one was open for 0% of the time, Pallas kernels for 21%

profile of v3, /device:TPU:1, one launch (start us, length us, event | category | flops | bytes accessed | tf_op | source)
XLA Modules:
  0.0 89.2 jit_solution(4727570303005445971)
XLA Ops:
  0.6 4.3 %first.1 = (s32[344]{0:T(512)}, f32[10,128,128]{2,1,0:T(8,128)}, f32[10,128,128]{2,1,0:T(8,128)}, f32[8,128,128]{2,1,0:T(8,128)}, f32[8,128,128]{2,1,0:T(8,128)}, /*index=5*/f32[2,128,128]{2,1,0:T(8,128)}) custom-call(s32[12,512]{1,0:T(8,128)} %bitcast.12, f32[48,128,128]{2,1,0:T(8,128)} %bitcast.5), custom_call_target="tpu_custom_call" | custom-call | bytes 10485760 | tf_op jit(solution)/shard_map/first/pallas_call | solution.py:473
  4.9 2.8 %collective-permute-start = (f32[2,128,128]{2,1,0:T(8,128)}, f32[2,128,128]{2,1,0:T(8,128)S(1)}, u32[]{:S(2)}, u32[]{:S(2)}) collective-permute-start(f32[2,128,128]{2,1,0:T(8,128)} %get-tuple-element.26), channel_id=1, source_target_pairs={{120,0},{121,1},{122,2},{123,3},{124,4},{125,5},{126,6},{127,7},{1... | collective-permute-start | bytes 393224 | tf_op jit(solution)/shard_map/ppermute | solution.py:482
  7.7 3.7 %collective-permute-start.1 = (f32[10,128,128]{2,1,0:T(8,128)}, f32[10,128,128]{2,1,0:T(8,128)S(1)}, u32[]{:S(2)}, u32[]{:S(2)}) collective-permute-start(f32[10,128,128]{2,1,0:T(8,128)} %get-tuple-element.30), channel_id=1, source_target_pairs={{15,0},{8,1},{9,2},{10,3},{11,4},{12,5},{13,6},{14,7},{7,8},{0,9},... | collective-permute-start | bytes 1966088 | tf_op jit(solution)/shard_map/ppermute | solution.py:479
  11.4 4.3 %collective-permute-start.2 = (f32[10,128,128]{2,1,0:T(8,128)}, f32[10,128,128]{2,1,0:T(8,128)S(1)}, u32[]{:S(2)}, u32[]{:S(2)}) collective-permute-start(f32[10,128,128]{2,1,0:T(8,128)} %get-tuple-element.31), channel_id=1, source_target_pairs={{9,0},{10,1},{11,2},{12,3},{13,4},{14,5},{15,6},{8,7},{1,8},{2,9},... | collective-permute-start | bytes 1966088 | tf_op jit(solution)/shard_map/ppermute | solution.py:478
  15.7 0.0 collective-permute-start.3
  15.7 6.3 %collective-permute-start.4 = (f32[8,128,128]{2,1,0:T(8,128)}, f32[8,128,128]{2,1,0:T(8,128)S(1)}, u32[]{:S(2)}, u32[]{:S(2)}) collective-permute-start(f32[8,128,128]{2,1,0:T(8,128)} %get-tuple-element.33), channel_id=1, source_target_pairs={{121,0},{122,1},{123,2},{124,3},{125,4},{126,5},{127,6},{120,7},{1... | collective-permute-start | bytes 1572872 | tf_op jit(solution)/shard_map/ppermute | solution.py:480
  21.9 0.0 collective-permute-done.after.beside
  22.0 0.0 copy-start.2
  22.0 0.7 copy-done.2
  22.6 8.1 %local.1 = (s32[344]{0:T(512)S(1)}, bf16[48,128,256]{2,1,0:T(8,128)(2,1)S(1)}, f32[48,128,128]{2,1,0:T(8,128)S(1)}) custom-call(s32[12,512]{1,0:T(8,128)S(1)} %bitcast.13, f32[48,128,128]{2,1,0:T(8,128)S(1)} %bitcast.6, s32[344]{0:T(512)S(1)} %copy-done.2, f32[2,128,128]{2,1,0:T(8,128)S(1)} %collective-permute-done.after.beside), custom_call_target="tpu_custom_call" | custom-call | flops 6710886400 | bytes 9437184 | tf_op jit(solution)/shard_map/local/pallas_call | solution.py:483
  30.8 0.0 slice-start.2
  30.8 0.7 late.1
  31.5 0.1 collective-permute-start.7
  31.6 2.8 %collective-permute-done.1.near_m.behind = f32[10,128,128]{2,1,0:T(8,128)S(1)} collective-permute-done((f32[10,128,128]{2,1,0:T(8,128)}, f32[10,128,128]{2,1,0:T(8,128)S(1)}, u32[]{:S(2)}, u32[]{:S(2)}) %collective-permute-start.1) | collective-permute-done | bytes 655392 | tf_op jit(solution)/shard_map/ppermute | solution.py:479
  34.4 3.2 %collective-permute-start.9 = (f32[10,128,128]{2,1,0:T(8,128)S(1)}, f32[10,128,128]{2,1,0:T(8,128)S(1)}, u32[]{:S(2)}, u32[]{:S(2)}) collective-permute-start(f32[10,128,128]{2,1,0:T(8,128)S(1)} %get-tuple-element.34.after), channel_id=1, source_target_pairs={{120,0},{121,1},{122,2},{123,3},{124,4},{125,5},{126,6},{127,7},{1... | collective-permute-start | bytes 1966088 | tf_op jit(solution)/shard_map/ppermute | solution.py:500
  37.6 2.1 %collective-permute-done.2.near_p.ahead = f32[10,128,128]{2,1,0:T(8,128)S(1)} collective-permute-done((f32[10,128,128]{2,1,0:T(8,128)}, f32[10,128,128]{2,1,0:T(8,128)S(1)}, u32[]{:S(2)}, u32[]{:S(2)}) %collective-permute-start.2) | collective-permute-done | bytes 655392 | tf_op jit(solution)/shard_map/ppermute | solution.py:478
  39.8 2.0 %collective-permute-start.8 = (f32[10,128,128]{2,1,0:T(8,128)S(1)}, f32[10,128,128]{2,1,0:T(8,128)S(1)}, u32[]{:S(2)}, u32[]{:S(2)}) collective-permute-start(f32[10,128,128]{2,1,0:T(8,128)S(1)} %get-tuple-element.35.also), channel_id=1, source_target_pairs={{1,0},{2,1},{3,2},{4,3},{5,4},{6,5},{7,6},{0,7},{9,8},{10,9},{11,1... | collective-permute-start | bytes 1966088 | tf_op jit(solution)/shard_map/ppermute | solution.py:496
  41.8 0.6 second.1
  42.4 0.0 collective-permute-done.3.far_m
  42.4 3.9 %collective-permute-start.5 = (f32[8,128,128]{2,1,0:T(8,128)S(1)}, f32[8,128,128]{2,1,0:T(8,128)S(1)}, u32[]{:S(2)}, u32[]{:S(2)}) collective-permute-start(f32[8,128,128]{2,1,0:T(8,128)S(1)} %get-tuple-element.38), channel_id=1, source_target_pairs={{8,0},{9,1},{10,2},{11,3},{12,4},{13,5},{14,6},{15,7},{0,8},{1,9},... | collective-permute-start | bytes 1572872 | tf_op jit(solution)/shard_map/ppermute | solution.py:498
  46.3 0.0 collective-permute-done.4.far_p
  46.3 0.3 collective-permute-start.6
  46.6 2.9 %early.1 = (bf16[16,128,256]{2,1,0:T(8,128)(2,1)S(1)}, bf16[24,128,256]{2,1,0:T(8,128)(2,1)S(1)}, f32[48,128,128]{2,1,0:T(8,128)S(1)}) custom-call(s32[344]{0:T(512)S(1)} %get-tuple-element.27.tab, bf16[48,128,256]{2,1,0:T(8,128)(2,1)S(1)} %get-tuple-element.28.wide, f32[48,128,128]{2,1,0:T(8,128)S(1)} %get-tuple-element.29.refs_0_.square_in, ...), custom_call_target="tpu_custom_call" | custom-call | tf_op jit(solution)/shard_map/early/pallas_call | solution.py:501
  49.5 0.0 collective-permute-done.5.low
  49.5 0.0 collective-permute-done.6.high
  49.5 6.5 %pair.1 = (bf16[16,128,256]{2,1,0:T(8,128)(2,1)S(1)}, bf16[10,128,256]{2,1,0:T(8,128)(2,1)S(1)}, f32[48,128,128]{2,1,0:T(8,128)S(1)}, f32[48,128,128]{2,1,0:T(8,128)S(1)}) custom-call(s32[344]{0:T(512)S(1)} %get-tuple-element.27.tab, bf16[48,128,256]{2,1,0:T(8,128)(2,1)S(1)} %get-tuple-element.28.wide, f32[48,128,128]{2,1,0:T(8,128)S(1)} %get-tuple-element.37.square_in, ...), custom_call_target="tpu_custom_call" | custom-call | tf_op jit(solution)/shard_map/pair/pallas_call | solution.py:507
  55.9 0.0 collective-permute-done.7.behind
  56.0 0.6 collective-permute-done.8.ahead
  56.5 9.1 %final.1 = (f32[4,12,128,128]{3,2,1,0:T(8,128)}, f32[128,128]{1,0:T(8,128)S(1)}) custom-call(s32[344]{0:T(512)S(1)} %get-tuple-element.27.tab, bf16[48,128,256]{2,1,0:T(8,128)(2,1)S(1)} %get-tuple-element.28.wide, bf16[16,128,256]{2,1,0:T(8,128)(2,1)S(1)} %get-tuple-element.36.own_early, bf16[16,128,256]{2,1,0:T(8,128)(2,1)S(1)} %get-tuple-element.40.own_late, ...), custom_call_target="tpu_custom_call" | custom-call | flops 3355443200 | bytes 31457280 | tf_op jit(solution)/shard_map/final/pallas_call | solution.py:513
  65.7 22.7 %all_to_all.9 = f32[128,1,128]{2,1,0:T(1,128)S(1)} all-to-all(f32[128,1,128]{2,1,0:T(1,128)S(1)} %bitcast.11), channel_id=1, replica_groups=mesh['row'=16,'col'=8] {'row','col'}, dimensions={0} | all-to-all | bytes 131072 | tf_op jit(solution)/shard_map/all_to_all | solution.py:525
  88.4 0.2 reduce_sum.9
  88.5 0.7 mul.8
  (14 shorter events, 0.0 us)
Async XLA Ops:
  0.6 21.3 %copy-start.1 = (s32[512,12]{0,1:T(8,128)S(1)}, s32[512,12]{0,1:T(8,128)}, u32[]{:S(2)}) copy-start(s32[512,12]{0,1:T(8,128)} %param.4) | copy-start | bytes 73732
  0.6 21.3 %copy-start = (f32[4,12,128,128]{3,2,1,0:T(8,128)S(1)}, f32[4,12,128,128]{3,2,1,0:T(8,128)}, u32[]{:S(2)}) copy-start(f32[4,12,128,128]{3,2,1,0:T(8,128)} %param.3) | copy-start | bytes 9437188
  4.9 17.0 %collective-permute-start = (f32[2,128,128]{2,1,0:T(8,128)}, f32[2,128,128]{2,1,0:T(8,128)S(1)}, u32[]{:S(2)}, u32[]{:S(2)}) collective-permute-start(f32[2,128,128]{2,1,0:T(8,128)} %get-tuple-element.26), channel_id=1, source_target_pairs={{120,0},{121,1},{122,2},{123,3},{124,4},{125,5},{126,6},{127,7},{1... | collective-permute-start | bytes 393224 | tf_op jit(solution)/shard_map/ppermute | solution.py:482
  7.7 26.7 %collective-permute-start.1 = (f32[10,128,128]{2,1,0:T(8,128)}, f32[10,128,128]{2,1,0:T(8,128)S(1)}, u32[]{:S(2)}, u32[]{:S(2)}) collective-permute-start(f32[10,128,128]{2,1,0:T(8,128)} %get-tuple-element.30), channel_id=1, source_target_pairs={{15,0},{8,1},{9,2},{10,3},{11,4},{12,5},{13,6},{14,7},{7,8},{0,9},... | collective-permute-start | bytes 1966088 | tf_op jit(solution)/shard_map/ppermute | solution.py:479
  11.4 28.4 %collective-permute-start.2 = (f32[10,128,128]{2,1,0:T(8,128)}, f32[10,128,128]{2,1,0:T(8,128)S(1)}, u32[]{:S(2)}, u32[]{:S(2)}) collective-permute-start(f32[10,128,128]{2,1,0:T(8,128)} %get-tuple-element.31), channel_id=1, source_target_pairs={{9,0},{10,1},{11,2},{12,3},{13,4},{14,5},{15,6},{8,7},{1,8},{2,9},... | collective-permute-start | bytes 1966088 | tf_op jit(solution)/shard_map/ppermute | solution.py:478
  15.7 26.7 %collective-permute-start.3 = (f32[8,128,128]{2,1,0:T(8,128)}, f32[8,128,128]{2,1,0:T(8,128)S(1)}, u32[]{:S(2)}, u32[]{:S(2)}) collective-permute-start(f32[8,128,128]{2,1,0:T(8,128)} %get-tuple-element.32), channel_id=1, source_target_pairs={{127,0},{120,1},{121,2},{122,3},{123,4},{124,5},{125,6},{126,7},{2... | collective-permute-start | bytes 1572872 | tf_op jit(solution)/shard_map/ppermute | solution.py:481
  15.7 30.6 %collective-permute-start.4 = (f32[8,128,128]{2,1,0:T(8,128)}, f32[8,128,128]{2,1,0:T(8,128)S(1)}, u32[]{:S(2)}, u32[]{:S(2)}) collective-permute-start(f32[8,128,128]{2,1,0:T(8,128)} %get-tuple-element.33), channel_id=1, source_target_pairs={{121,0},{122,1},{123,2},{124,3},{125,4},{126,5},{127,6},{120,7},{1... | collective-permute-start | bytes 1572872 | tf_op jit(solution)/shard_map/ppermute | solution.py:480
  22.0 0.7 copy-start.2
  22.6 33.9 %slice-start = ((s8[14155776]{0:T(1024)(128)(4,1)}), s8[4194304]{0:T(1024)(128)(4,1)S(1)}, s32[]{:S(2)}) async-start(s8[14155776]{0:T(1024)(128)(4,1)} %bitcast.9), calls=%async_computation.1 | async-start | bytes 8388608
  22.6 33.9 %slice-start.1 = ((s8[14155776]{0:T(1024)(128)(4,1)}), s8[4194304]{0:T(1024)(128)(4,1)S(1)}, s32[]{:S(2)}) async-start(s8[14155776]{0:T(1024)(128)(4,1)} %bitcast.9), calls=%async_computation.2 | async-start | bytes 8388608
  30.8 25.7 %slice-start.2 = ((s8[14155776]{0:T(1024)(128)(4,1)}), s8[4194304]{0:T(1024)(128)(4,1)S(1)}, s32[]{:S(2)}) async-start(s8[14155776]{0:T(1024)(128)(4,1)} %bitcast.9), calls=%async_computation.3 | async-start | bytes 8388608
  31.5 24.4 %collective-permute-start.7 = (f32[10,128,128]{2,1,0:T(8,128)S(1)}, f32[10,128,128]{2,1,0:T(8,128)S(1)}, u32[]{:S(2)}, u32[]{:S(2)}) collective-permute-start(f32[10,128,128]{2,1,0:T(8,128)S(1)} %get-tuple-element.45), channel_id=1, source_target_pairs={{7,0},{0,1},{1,2},{2,3},{3,4},{4,5},{5,6},{6,7},{15,8},{8,9},{9,10... | collective-permute-start | bytes 1966088 | tf_op jit(solution)/shard_map/ppermute | solution.py:497
  34.4 21.6 %collective-permute-start.9 = (f32[10,128,128]{2,1,0:T(8,128)S(1)}, f32[10,128,128]{2,1,0:T(8,128)S(1)}, u32[]{:S(2)}, u32[]{:S(2)}) collective-permute-start(f32[10,128,128]{2,1,0:T(8,128)S(1)} %get-tuple-element.34.after), channel_id=1, source_target_pairs={{120,0},{121,1},{122,2},{123,3},{124,4},{125,5},{126,6},{127,7},{1... | collective-permute-start | bytes 1966088 | tf_op jit(solution)/shard_map/ppermute | solution.py:500
  39.8 16.7 %collective-permute-start.8 = (f32[10,128,128]{2,1,0:T(8,128)S(1)}, f32[10,128,128]{2,1,0:T(8,128)S(1)}, u32[]{:S(2)}, u32[]{:S(2)}) collective-permute-start(f32[10,128,128]{2,1,0:T(8,128)S(1)} %get-tuple-element.35.also), channel_id=1, source_target_pairs={{1,0},{2,1},{3,2},{4,3},{5,4},{6,5},{7,6},{0,7},{9,8},{10,9},{11,1... | collective-permute-start | bytes 1966088 | tf_op jit(solution)/shard_map/ppermute | solution.py:496
  42.4 7.0 %collective-permute-start.5 = (f32[8,128,128]{2,1,0:T(8,128)S(1)}, f32[8,128,128]{2,1,0:T(8,128)S(1)}, u32[]{:S(2)}, u32[]{:S(2)}) collective-permute-start(f32[8,128,128]{2,1,0:T(8,128)S(1)} %get-tuple-element.38), channel_id=1, source_target_pairs={{8,0},{9,1},{10,2},{11,3},{12,4},{13,5},{14,6},{15,7},{0,8},{1,9},... | collective-permute-start | bytes 1572872 | tf_op jit(solution)/shard_map/ppermute | solution.py:498
  46.3 3.2 %collective-permute-start.6 = (f32[8,128,128]{2,1,0:T(8,128)S(1)}, f32[8,128,128]{2,1,0:T(8,128)S(1)}, u32[]{:S(2)}, u32[]{:S(2)}) collective-permute-start(f32[8,128,128]{2,1,0:T(8,128)S(1)} %get-tuple-element.39), channel_id=1, source_target_pairs={{8,0},{9,1},{10,2},{11,3},{12,4},{13,5},{14,6},{15,7},{0,8},{1,9},... | collective-permute-start | bytes 1572872 | tf_op jit(solution)/shard_map/ppermute | solution.py:499
  46.6 9.9 %slice-start.3 = ((s8[14155776]{0:T(1024)(128)(4,1)}), s8[1572864]{0:T(1024)(128)(4,1)S(1)}, s32[]{:S(2)}) async-start(s8[14155776]{0:T(1024)(128)(4,1)} %bitcast.9), calls=%async_computation.4 | async-start | bytes 3145728

commit v4 on v3

--- a/solution.py
+++ b/solution.py
@@ -115,16 +115,20 @@
 
 
 def first_kernel(pat_in, dens_in, tab, near_m, near_p, far_m, far_p, beside, dens, pat, sem):
-    load = pltpu.make_async_copy(dens_in, dens, sem.at[0])
-    load.start()
-    pat_load = pltpu.make_async_copy(pat_in, pat, sem.at[1])
+    pat_load = pltpu.make_async_copy(pat_in, pat, sem.at[OWN])
     pat_load.start()
+    loads = []
+    for g in range(OWN):
+        rows = pl.ds(g * SLOTS, SLOTS)
+        loads.append(pltpu.make_async_copy(dens_in.at[rows], dens.at[rows], sem.at[g]))
+        loads[g].start()
     pat_load.wait()
     row = lax.axis_index("row")
     col = lax.axis_index("col")
     own_table(pat, row, col, tab)
     send_table(pat, row, col, tab)
-    load.wait()
+    for load in loads:
+        load.wait()
     for out, f, edge in ((near_m, 5, 3), (near_p, 7, 4)):
         fill(out, tab, dens, f)
         for k in range(2):
@@ -262,10 +266,13 @@
 
 EARLY = (0, 2, 5, 7)
 PAIR = (6,)
-LATE = (3, 4, 1)
+BEHIND = (3,)
+LATE = (4, 1)
 EARLY_AT, N_EARLY = offsets(EARLY)
 PAIR_AT, N_PAIR = offsets(PAIR)
 LATE_AT, N_LATE = offsets(LATE)
+BEHIND_AT, N_BEHIND = offsets(BEHIND)
+READY = 5
 
 
 def widen(ref, start, out, at, count):
@@ -319,7 +326,7 @@
     widen(high, 0, pair, 6, 4)
 
     def rows(g, _):
-        back = own_terms(tab, g, PAIR + LATE)
+        back = own_terms(tab, g, PAIR + BEHIND + LATE)
         terms = far_terms(tab, g, PAIR, PAIR_AT, no_terms())
         lefts = lambda left: wide[g * SLOTS + left]
         for i, (left, number, index) in enumerate(back):
@@ -346,17 +353,47 @@
     lax.fori_loop(0, OWN, rows, 0)
 
 
-def final_kernel(tab, wide, own_early, own_late, early, pair, square, cube, behind, ahead, beside, ham,
+def behind_kernel(tab, wide, square_in, cube_in, own_early, early, ref, behind, square, cube, zeros):
+    zeros[...] = jnp.zeros_like(zeros)
+    widen(ref, 0, behind, 0, N_BEHIND)
+
+    def rows(g, _):
+        terms = far_terms(tab, g, BEHIND, BEHIND_AT, no_terms())
+        lefts = lambda left: wide[g * SLOTS + left]
+        for o in range(SLOTS):
+            value = square_in[g * SLOTS + o]
+            if o >= OWN and terms[o]:
+                value = value + halves(chain(None, terms[o], lefts, behind, zeros))
+            square[g * SLOTS + o] = value
+        left = split(square[g * SLOTS + OWN + READY])
+        ((_, number, index),) = own_terms(tab, g, (READY,))
+        ready = far_terms(tab, g, (READY,), EARLY_AT, no_terms())
+        for o in range(SLOTS):
+            value = cube_in[g * SLOTS + o]
+            if o >= OWN and ready[o]:
+                value = value + halves(chain(None, ready[o], lambda _: left, early, zeros))
+            cube[g * SLOTS + o] = value
+        at = g * SLOTS + number
+        cube[at] = cube[at] + halves(product(left, own_early[index]))
+        return 0
+
+    lax.fori_loop(0, OWN, rows, 0)
+
+
+def final_kernel(tab, wide, own_early, own_late, early, pair, behind, square, cube, ahead, beside, ham,
                  purified, virial, late, far_square, wsq, own_cube, back_buf, out_buf, sums, zeros, out_sem):
     zeros[...] = jnp.zeros_like(zeros)
     sums[...] = jnp.zeros_like(sums)
-    for d, ref in ((3, behind), (4, ahead), (1, beside)):
+    for d, ref in ((4, ahead), (1, beside)):
         widen(ref, 0, late, LATE_AT[d], 10)
 
     def squares(g, _):
         terms = far_terms(tab, g, LATE, LATE_AT, no_terms())
         lefts = lambda left: wide[g * SLOTS + left]
-        sums_of = [halves(chain(None, terms[o], lefts, late, zeros)) for o in range(OWN, SLOTS)]
+        sums_of = [
+            halves(chain(None, terms[o], lefts, late, zeros)) if terms[o] else 0.0
+            for o in range(OWN, SLOTS)
+        ]
         for i, total in enumerate(sums_of):
             value = square[g * SLOTS + OWN + i] + total
             far_square[g * 8 + i] = value
@@ -367,7 +404,9 @@
 
     def rows(g, _):
         terms = far_terms(tab, g, PAIR, PAIR_AT, no_terms())
-        early_terms = far_terms(tab, g, EARLY, EARLY_AT, no_terms())
+        rest = tuple(d for d in EARLY if d != READY)
+        early_terms = far_terms(tab, g, rest, EARLY_AT, no_terms())
+        behind_terms = far_terms(tab, g, BEHIND, BEHIND_AT, no_terms())
         late_terms = far_terms(tab, g, LATE, LATE_AT, no_terms())
         lefts = lambda left: wsq[g * 8 + left - OWN]
 
@@ -378,10 +417,10 @@
                 part = ham[c, g, slot].astype(jnp.float32) * value
                 sums[c] += jnp.sum(part.reshape(EDGE // 8, 8, EDGE), axis=0)
 
-        back = own_terms(tab, g, EARLY) + own_terms(tab, g, PAIR + LATE)
+        back = own_terms(tab, g, rest) + own_terms(tab, g, PAIR + BEHIND + LATE)
         backs = []
         for i, (left, number, index) in enumerate(back):
-            own = own_early if i < len(EARLY) else own_late
+            own = own_early if i < len(rest) else own_late
             backs.append(halves(product(lefts(left), own[index])))
         cubes = []
         for o in range(OWN, SLOTS):
@@ -390,6 +429,7 @@
                     back_buf[i] = total
             total = chain(None, terms[o], lefts, pair, zeros)
             total = chain(total, early_terms[o], lefts, early, zeros)
+            total = chain(total, behind_terms[o], lefts, behind, zeros)
             total = chain(total, late_terms[o], lefts, late, zeros)
             cubes.append(halves(total))
         for i, total in enumerate(cubes):
@@ -473,7 +513,7 @@
     tab, near_m, near_p, far_m, far_p, beside_own = call(
         first_kernel, "first", (table, blocks(10), blocks(10), blocks(8), blocks(8), blocks(2)),
         [HBM, HBM], (SMEM,) + (VMEM,) * 5,
-        [scratch(OWN * SLOTS), pltpu.SMEM((SLOTS, N_DEV * OWN), jnp.int32), dma((2,))], 0, 10, 56,
+        [scratch(OWN * SLOTS), pltpu.SMEM((SLOTS, N_DEV * OWN), jnp.int32), dma((OWN + 1,))], 0, 10, 56,
     )(pattern.T, dens)
     near_ahead = lax.ppermute(near_m, AXES, from_direction(7))
     near_behind = lax.ppermute(near_p, AXES, from_direction(5))
@@ -510,6 +550,11 @@
         [SMEM] + [VMEM] * 5, (VMEM,) * 4,
         [scratch(8), wide_scratch(OWN), wide_scratch()], 0, 0,
     )(tab, wide, square, pair_low_in, pair_high_in, beside_own)
+    behind, square, cube = call(
+        behind_kernel, "behind",
+        (wides(N_BEHIND), blocks(OWN * SLOTS), blocks(OWN * SLOTS)),
+        [SMEM] + [VMEM] * 6, (VMEM,) * 3, [wide_scratch()], 0, 0,
+    )(tab, wide, square, cube, own_early, early, late_behind)
     purified, line = call(
         final_kernel, "final",
         (blocks(OWN, SLOTS), jax.ShapeDtypeStruct((N_DEV, EDGE), F32)),
@@ -518,7 +563,7 @@
             wide_scratch(N_LATE), scratch(8 * OWN), wide_scratch(8 * OWN), scratch(OWN), scratch(8),
             scratch(OWN, SLOTS), pltpu.VMEM((9, 8, EDGE), F32), wide_scratch(), dma((OWN,)),
         ], 200, 30,
-    )(tab, wide, own_early, own_late, early, pair, square, cube, late_behind, late_ahead, beside_in,
+    )(tab, wide, own_early, own_late, early, pair, behind, square, cube, late_ahead, beside_in,
       ham_strain)
     total_blocks = N_DEV * OWN
     factor = 1.0 / math.sqrt(float(total_blocks * SLOTS * EDGE * EDGE))

time: 89.3 us -> 88.7 us (level)
  blocking collectives: 22.7 us -> 20.7 us
  Pallas kernels: 32.2 us -> 34 us
    pallas_call x0 -> x1, Pallas kernels: none -> 2.4 us  [body(): call(behind_kernel, 'behind', (wides(N_BEHIND), blocks(OWN * SLOTS), bloc...]
    all_to_all x1, blocking collectives: 22.7 us -> 20.7 us  [body(): lines = lax.all_to_all(line, AXES, 0, 0, tiled=True)]
  transfers between devices with their start and end apart: 10 -> 10, of which waited for: 3 -> 2; matrix products, arithmetic and copies ran while one was open for 0% -> 0% of each run, Pallas kernels for 21% -> 24%
where the time goes in v4:
time: 88.7 us; the launch traced here: 88.6 us
  Pallas kernels  34 us (38%)
  starting transfers between devices  26.5 us (30%)
  blocking collectives  20.7 us (23%)
  waiting for transfers between devices  4.96 us (6%)
  local copies, waits for them, and re-layouts  1.37 us (2%)
    all_to_all x1, blocking collectives, body(): lines = lax.all_to_all(line, AXES, 0, 0, tiled=True)  20.7 us
    pallas_call x1, Pallas kernels, body(): call(final_kernel, 'final', (blocks(OWN, SLOTS), jax.ShapeDtypeStruct((N_...  8.5 us
    pallas_call x1, Pallas kernels, body(): call(local_kernel, 'local', (table, wides(OWN * SLOTS), blocks(OWN * SLOT...  8.15 us
    pallas_call x1, Pallas kernels, body(): call(pair_kernel, 'pair', (wides(16), wides(N_PAIR), blocks(OWN * SLOTS),...  6.45 us
    ppermute x1, starting transfers between devices, body(): far_ahead = lax.ppermute(far_m, AXES, from_direction(2))  6.26 us
    pallas_call x1, Pallas kernels, body(): call(first_kernel, 'first', (table, blocks(10), blocks(10), blocks(8), bl...  4.29 us
    ppermute x1, starting transfers between devices, body(): near_ahead = lax.ppermute(near_m, AXES, from_direction(7))  4.29 us
    ppermute x1, starting transfers between devices, body(): pair_low_in = lax.ppermute(pair_low, AXES, from_direction(6))  3.87 us
  transfers between devices with their start and end apart: 10, of which 2 were waited for; matrix products, arithmetic and copies ran while one was open for 0% of the time, Pallas kernels for 24%

profile of v4, /device:TPU:1, one launch (start us, length us, event | category | flops | bytes accessed | tf_op | source)
XLA Modules:
  0.0 88.6 jit_solution(6843690337133295059)
XLA Ops:
  0.6 4.3 %first.1 = (s32[344]{0:T(512)}, f32[10,128,128]{2,1,0:T(8,128)}, f32[10,128,128]{2,1,0:T(8,128)}, f32[8,128,128]{2,1,0:T(8,128)}, f32[8,128,128]{2,1,0:T(8,128)}, /*index=5*/f32[2,128,128]{2,1,0:T(8,128)}) custom-call(s32[12,512]{1,0:T(8,128)} %bitcast.12, f32[48,128,128]{2,1,0:T(8,128)} %bitcast.5), custom_call_target="tpu_custom_call" | custom-call | bytes 10485760 | tf_op jit(solution)/shard_map/first/pallas_call | solution.py:513
  4.9 2.8 %collective-permute-start = (f32[2,128,128]{2,1,0:T(8,128)}, f32[2,128,128]{2,1,0:T(8,128)S(1)}, u32[]{:S(2)}, u32[]{:S(2)}) collective-permute-start(f32[2,128,128]{2,1,0:T(8,128)} %get-tuple-element.29), channel_id=1, source_target_pairs={{120,0},{121,1},{122,2},{123,3},{124,4},{125,5},{126,6},{127,7},{1... | collective-permute-start | bytes 393224 | tf_op jit(solution)/shard_map/ppermute | solution.py:522
  7.7 3.7 %collective-permute-start.1 = (f32[10,128,128]{2,1,0:T(8,128)}, f32[10,128,128]{2,1,0:T(8,128)S(1)}, u32[]{:S(2)}, u32[]{:S(2)}) collective-permute-start(f32[10,128,128]{2,1,0:T(8,128)} %get-tuple-element.33), channel_id=1, source_target_pairs={{15,0},{8,1},{9,2},{10,3},{11,4},{12,5},{13,6},{14,7},{7,8},{0,9},... | collective-permute-start | bytes 1966088 | tf_op jit(solution)/shard_map/ppermute | solution.py:519
  11.4 4.3 %collective-permute-start.2 = (f32[10,128,128]{2,1,0:T(8,128)}, f32[10,128,128]{2,1,0:T(8,128)S(1)}, u32[]{:S(2)}, u32[]{:S(2)}) collective-permute-start(f32[10,128,128]{2,1,0:T(8,128)} %get-tuple-element.34), channel_id=1, source_target_pairs={{9,0},{10,1},{11,2},{12,3},{13,4},{14,5},{15,6},{8,7},{1,8},{2,9},... | collective-permute-start | bytes 1966088 | tf_op jit(solution)/shard_map/ppermute | solution.py:518
  15.7 0.0 collective-permute-start.3
  15.7 6.3 %collective-permute-start.4 = (f32[8,128,128]{2,1,0:T(8,128)}, f32[8,128,128]{2,1,0:T(8,128)S(1)}, u32[]{:S(2)}, u32[]{:S(2)}) collective-permute-start(f32[8,128,128]{2,1,0:T(8,128)} %get-tuple-element.36), channel_id=1, source_target_pairs={{121,0},{122,1},{123,2},{124,3},{125,4},{126,5},{127,6},{120,7},{1... | collective-permute-start | bytes 1572872 | tf_op jit(solution)/shard_map/ppermute | solution.py:520
  22.0 0.0 collective-permute-done.after.beside
  22.0 0.0 copy-start.2
  22.0 0.7 copy-done.2
  22.7 8.2 %local.1 = (s32[344]{0:T(512)S(1)}, bf16[48,128,256]{2,1,0:T(8,128)(2,1)S(1)}, f32[48,128,128]{2,1,0:T(8,128)S(1)}) custom-call(s32[12,512]{1,0:T(8,128)S(1)} %bitcast.13, f32[48,128,128]{2,1,0:T(8,128)S(1)} %bitcast.6, s32[344]{0:T(512)S(1)} %copy-done.2, f32[2,128,128]{2,1,0:T(8,128)S(1)} %collective-permute-done.after.beside), custom_call_target="tpu_custom_call" | custom-call | flops 6710886400 | bytes 9437184 | tf_op jit(solution)/shard_map/local/pallas_call | solution.py:523
  30.8 0.7 late.1
  31.5 0.1 collective-permute-start.7
  31.6 2.8 %collective-permute-done.1.near_m.behind = f32[10,128,128]{2,1,0:T(8,128)S(1)} collective-permute-done((f32[10,128,128]{2,1,0:T(8,128)}, f32[10,128,128]{2,1,0:T(8,128)S(1)}, u32[]{:S(2)}, u32[]{:S(2)}) %collective-permute-start.1) | collective-permute-done | bytes 655392 | tf_op jit(solution)/shard_map/ppermute | solution.py:519
  34.4 3.2 %collective-permute-start.9 = (f32[10,128,128]{2,1,0:T(8,128)S(1)}, f32[10,128,128]{2,1,0:T(8,128)S(1)}, u32[]{:S(2)}, u32[]{:S(2)}) collective-permute-start(f32[10,128,128]{2,1,0:T(8,128)S(1)} %get-tuple-element.37.after), channel_id=1, source_target_pairs={{120,0},{121,1},{122,2},{123,3},{124,4},{125,5},{126,6},{127,7},{1... | collective-permute-start | bytes 1966088 | tf_op jit(solution)/shard_map/ppermute | solution.py:540
  37.7 2.1 %collective-permute-done.2.near_p.ahead = f32[10,128,128]{2,1,0:T(8,128)S(1)} collective-permute-done((f32[10,128,128]{2,1,0:T(8,128)}, f32[10,128,128]{2,1,0:T(8,128)S(1)}, u32[]{:S(2)}, u32[]{:S(2)}) %collective-permute-start.2) | collective-permute-done | bytes 655392 | tf_op jit(solution)/shard_map/ppermute | solution.py:518
  39.8 2.0 %collective-permute-start.8 = (f32[10,128,128]{2,1,0:T(8,128)S(1)}, f32[10,128,128]{2,1,0:T(8,128)S(1)}, u32[]{:S(2)}, u32[]{:S(2)}) collective-permute-start(f32[10,128,128]{2,1,0:T(8,128)S(1)} %get-tuple-element.38.also), channel_id=1, source_target_pairs={{1,0},{2,1},{3,2},{4,3},{5,4},{6,5},{7,6},{0,7},{9,8},{10,9},{11,1... | collective-permute-start | bytes 1966088 | tf_op jit(solution)/shard_map/ppermute | solution.py:536
  41.8 0.6 second.1
  42.5 0.0 collective-permute-done.3.far_m
  42.5 3.9 %collective-permute-start.5 = (f32[8,128,128]{2,1,0:T(8,128)S(1)}, f32[8,128,128]{2,1,0:T(8,128)S(1)}, u32[]{:S(2)}, u32[]{:S(2)}) collective-permute-start(f32[8,128,128]{2,1,0:T(8,128)S(1)} %get-tuple-element.41), channel_id=1, source_target_pairs={{8,0},{9,1},{10,2},{11,3},{12,4},{13,5},{14,6},{15,7},{0,8},{1,9},... | collective-permute-start | bytes 1572872 | tf_op jit(solution)/shard_map/ppermute | solution.py:538
  46.3 0.0 collective-permute-done.4.far_p
  46.3 0.3 collective-permute-start.6
  46.6 2.9 %early.1 = (bf16[16,128,256]{2,1,0:T(8,128)(2,1)S(1)}, bf16[24,128,256]{2,1,0:T(8,128)(2,1)S(1)}, f32[48,128,128]{2,1,0:T(8,128)S(1)}) custom-call(s32[344]{0:T(512)S(1)} %get-tuple-element.30.tab, bf16[48,128,256]{2,1,0:T(8,128)(2,1)S(1)} %get-tuple-element.31.wide, f32[48,128,128]{2,1,0:T(8,128)S(1)} %get-tuple-element.32.refs_0_.square_in, ...), custom_call_target="tpu_custom_call" | custom-call | tf_op jit(solution)/shard_map/early/pallas_call | solution.py:541
  49.5 0.0 collective-permute-done.5.low
  49.5 0.0 slice-start.2
  49.5 6.5 %pair.1 = (bf16[16,128,256]{2,1,0:T(8,128)(2,1)S(1)}, bf16[10,128,256]{2,1,0:T(8,128)(2,1)S(1)}, f32[48,128,128]{2,1,0:T(8,128)S(1)}, f32[48,128,128]{2,1,0:T(8,128)S(1)}) custom-call(s32[344]{0:T(512)S(1)} %get-tuple-element.30.tab, bf16[48,128,256]{2,1,0:T(8,128)(2,1)S(1)} %get-tuple-element.31.wide, f32[48,128,128]{2,1,0:T(8,128)S(1)} %get-tuple-element.40.square_in, ...), custom_call_target="tpu_custom_call" | custom-call | tf_op jit(solution)/shard_map/pair/pallas_call | solution.py:547
  56.0 0.0 slice-start.3
  56.0 2.4 %behind.1 = (bf16[10,128,256]{2,1,0:T(8,128)(2,1)S(1)}, f32[48,128,128]{2,1,0:T(8,128)S(1)}, f32[48,128,128]{2,1,0:T(8,128)S(1)}) custom-call(s32[344]{0:T(512)S(1)} %get-tuple-element.30.tab, bf16[48,128,256]{2,1,0:T(8,128)(2,1)S(1)} %get-tuple-element.31.wide, f32[48,128,128]{2,1,0:T(8,128)S(1)} %get-tuple-element.46.square_in, ...), custom_call_target="tpu_custom_call" | custom-call | tf_op jit(solution)/shard_map/behind/pallas_call | solution.py:553
  58.4 0.0 collective-permute-done.9.beside
  58.5 8.5 %final.1 = (f32[4,12,128,128]{3,2,1,0:T(8,128)}, f32[128,128]{1,0:T(8,128)S(1)}) custom-call(s32[344]{0:T(512)S(1)} %get-tuple-element.30.tab, bf16[48,128,256]{2,1,0:T(8,128)(2,1)S(1)} %get-tuple-element.31.wide, bf16[16,128,256]{2,1,0:T(8,128)(2,1)S(1)} %get-tuple-element.39.own_early, bf16[16,128,256]{2,1,0:T(8,128)(2,1)S(1)} %get-tuple-element.43.own_late, ...), custom_call_target="tpu_custom_call" | custom-call | flops 3355443200 | bytes 31457280 | tf_op jit(solution)/shard_map/final/pallas_call | solution.py:558
  67.0 20.7 %all_to_all.9 = f32[128,1,128]{2,1,0:T(1,128)S(1)} all-to-all(f32[128,1,128]{2,1,0:T(1,128)S(1)} %bitcast.11), channel_id=1, replica_groups=mesh['row'=16,'col'=8] {'row','col'}, dimensions={0} | all-to-all | bytes 131072 | tf_op jit(solution)/shard_map/all_to_all | solution.py:570
  87.8 0.2 reduce_sum.9
  87.9 0.7 mul.8
  (15 shorter events, 0.0 us)
Async XLA Ops:
  0.6 21.4 %copy-start.1 = (s32[512,12]{0,1:T(8,128)S(1)}, s32[512,12]{0,1:T(8,128)}, u32[]{:S(2)}) copy-start(s32[512,12]{0,1:T(8,128)} %param.4) | copy-start | bytes 73732
  0.6 21.4 %copy-start = (f32[4,12,128,128]{3,2,1,0:T(8,128)S(1)}, f32[4,12,128,128]{3,2,1,0:T(8,128)}, u32[]{:S(2)}) copy-start(f32[4,12,128,128]{3,2,1,0:T(8,128)} %param.3) | copy-start | bytes 9437188
  4.9 17.0 %collective-permute-start = (f32[2,128,128]{2,1,0:T(8,128)}, f32[2,128,128]{2,1,0:T(8,128)S(1)}, u32[]{:S(2)}, u32[]{:S(2)}) collective-permute-start(f32[2,128,128]{2,1,0:T(8,128)} %get-tuple-element.29), channel_id=1, source_target_pairs={{120,0},{121,1},{122,2},{123,3},{124,4},{125,5},{126,6},{127,7},{1... | collective-permute-start | bytes 393224 | tf_op jit(solution)/shard_map/ppermute | solution.py:522
  7.7 26.7 %collective-permute-start.1 = (f32[10,128,128]{2,1,0:T(8,128)}, f32[10,128,128]{2,1,0:T(8,128)S(1)}, u32[]{:S(2)}, u32[]{:S(2)}) collective-permute-start(f32[10,128,128]{2,1,0:T(8,128)} %get-tuple-element.33), channel_id=1, source_target_pairs={{15,0},{8,1},{9,2},{10,3},{11,4},{12,5},{13,6},{14,7},{7,8},{0,9},... | collective-permute-start | bytes 1966088 | tf_op jit(solution)/shard_map/ppermute | solution.py:519
  11.4 28.4 %collective-permute-start.2 = (f32[10,128,128]{2,1,0:T(8,128)}, f32[10,128,128]{2,1,0:T(8,128)S(1)}, u32[]{:S(2)}, u32[]{:S(2)}) collective-permute-start(f32[10,128,128]{2,1,0:T(8,128)} %get-tuple-element.34), channel_id=1, source_target_pairs={{9,0},{10,1},{11,2},{12,3},{13,4},{14,5},{15,6},{8,7},{1,8},{2,9},... | collective-permute-start | bytes 1966088 | tf_op jit(solution)/shard_map/ppermute | solution.py:518
  15.7 26.7 %collective-permute-start.3 = (f32[8,128,128]{2,1,0:T(8,128)}, f32[8,128,128]{2,1,0:T(8,128)S(1)}, u32[]{:S(2)}, u32[]{:S(2)}) collective-permute-start(f32[8,128,128]{2,1,0:T(8,128)} %get-tuple-element.35), channel_id=1, source_target_pairs={{127,0},{120,1},{121,2},{122,3},{123,4},{124,5},{125,6},{126,7},{2... | collective-permute-start | bytes 1572872 | tf_op jit(solution)/shard_map/ppermute | solution.py:521
  15.7 30.6 %collective-permute-start.4 = (f32[8,128,128]{2,1,0:T(8,128)}, f32[8,128,128]{2,1,0:T(8,128)S(1)}, u32[]{:S(2)}, u32[]{:S(2)}) collective-permute-start(f32[8,128,128]{2,1,0:T(8,128)} %get-tuple-element.36), channel_id=1, source_target_pairs={{121,0},{122,1},{123,2},{124,3},{125,4},{126,5},{127,6},{120,7},{1... | collective-permute-start | bytes 1572872 | tf_op jit(solution)/shard_map/ppermute | solution.py:520
  22.0 0.7 copy-start.2
  31.5 24.5 %collective-permute-start.7 = (f32[10,128,128]{2,1,0:T(8,128)S(1)}, f32[10,128,128]{2,1,0:T(8,128)S(1)}, u32[]{:S(2)}, u32[]{:S(2)}) collective-permute-start(f32[10,128,128]{2,1,0:T(8,128)S(1)} %get-tuple-element.48), channel_id=1, source_target_pairs={{7,0},{0,1},{1,2},{2,3},{3,4},{4,5},{5,6},{6,7},{15,8},{8,9},{9,10... | collective-permute-start | bytes 1966088 | tf_op jit(solution)/shard_map/ppermute | solution.py:537
  34.4 24.0 %collective-permute-start.9 = (f32[10,128,128]{2,1,0:T(8,128)S(1)}, f32[10,128,128]{2,1,0:T(8,128)S(1)}, u32[]{:S(2)}, u32[]{:S(2)}) collective-permute-start(f32[10,128,128]{2,1,0:T(8,128)S(1)} %get-tuple-element.37.after), channel_id=1, source_target_pairs={{120,0},{121,1},{122,2},{123,3},{124,4},{125,5},{126,6},{127,7},{1... | collective-permute-start | bytes 1966088 | tf_op jit(solution)/shard_map/ppermute | solution.py:540
  39.8 18.6 %collective-permute-start.8 = (f32[10,128,128]{2,1,0:T(8,128)S(1)}, f32[10,128,128]{2,1,0:T(8,128)S(1)}, u32[]{:S(2)}, u32[]{:S(2)}) collective-permute-start(f32[10,128,128]{2,1,0:T(8,128)S(1)} %get-tuple-element.38.also), channel_id=1, source_target_pairs={{1,0},{2,1},{3,2},{4,3},{5,4},{6,5},{7,6},{0,7},{9,8},{10,9},{11,1... | collective-permute-start | bytes 1966088 | tf_op jit(solution)/shard_map/ppermute | solution.py:536
  42.5 7.0 %collective-permute-start.5 = (f32[8,128,128]{2,1,0:T(8,128)S(1)}, f32[8,128,128]{2,1,0:T(8,128)S(1)}, u32[]{:S(2)}, u32[]{:S(2)}) collective-permute-start(f32[8,128,128]{2,1,0:T(8,128)S(1)} %get-tuple-element.41), channel_id=1, source_target_pairs={{8,0},{9,1},{10,2},{11,3},{12,4},{13,5},{14,6},{15,7},{0,8},{1,9},... | collective-permute-start | bytes 1572872 | tf_op jit(solution)/shard_map/ppermute | solution.py:538
  46.3 3.2 %collective-permute-start.6 = (f32[8,128,128]{2,1,0:T(8,128)S(1)}, f32[8,128,128]{2,1,0:T(8,128)S(1)}, u32[]{:S(2)}, u32[]{:S(2)}) collective-permute-start(f32[8,128,128]{2,1,0:T(8,128)S(1)} %get-tuple-element.42), channel_id=1, source_target_pairs={{8,0},{9,1},{10,2},{11,3},{12,4},{13,5},{14,6},{15,7},{0,8},{1,9},... | collective-permute-start | bytes 1572872 | tf_op jit(solution)/shard_map/ppermute | solution.py:539
  46.6 11.8 %slice-start = ((s8[14155776]{0:T(1024)(128)(4,1)}), s8[4194304]{0:T(1024)(128)(4,1)S(1)}, s32[]{:S(2)}) async-start(s8[14155776]{0:T(1024)(128)(4,1)} %bitcast.9), calls=%async_computation.1 | async-start | bytes 8388608
  46.6 11.8 %slice-start.1 = ((s8[14155776]{0:T(1024)(128)(4,1)}), s8[4194304]{0:T(1024)(128)(4,1)S(1)}, s32[]{:S(2)}) async-start(s8[14155776]{0:T(1024)(128)(4,1)} %bitcast.9), calls=%async_computation.2 | async-start | bytes 8388608
  49.5 8.9 %slice-start.2 = ((s8[14155776]{0:T(1024)(128)(4,1)}), s8[4194304]{0:T(1024)(128)(4,1)S(1)}, s32[]{:S(2)}) async-start(s8[14155776]{0:T(1024)(128)(4,1)} %bitcast.9), calls=%async_computation.3 | async-start | bytes 8388608
  56.0 2.5 %slice-start.3 = ((s8[14155776]{0:T(1024)(128)(4,1)}), s8[1572864]{0:T(1024)(128)(4,1)S(1)}, s32[]{:S(2)}) async-start(s8[14155776]{0:T(1024)(128)(4,1)} %bitcast.9), calls=%async_computation.4 | async-start | bytes 3145728

commit v5 on v4

--- a/solution.py
+++ b/solution.py
@@ -1,3 +1,4 @@
+import functools
 import math
 
 import jax
@@ -138,8 +139,8 @@
     fill(beside, tab, dens, 1, 0, 2)
 
 
-def late_kernel(tab, dens, *refs):
-    for f, out in zip((3, 4, 1), refs[1:]):
+def late_kernel(dirs, tab, dens, *refs):
+    for f, out in zip(dirs, refs[1:]):
         fill(out, tab, dens, f, 2, 12)
 
 
@@ -413,6 +414,10 @@
         def finish(o, value):
             slot = tab[T_SLOT + g * SLOTS + o]
             out_buf[g, slot] = value
+            block = pltpu.make_async_copy(
+                out_buf.at[g, slot], purified.at[g, slot], out_sem.at[g]
+            )
+            block.start()
             for c in range(9):
                 part = ham[c, g, slot].astype(jnp.float32) * value
                 sums[c] += jnp.sum(part.reshape(EDGE // 8, 8, EDGE), axis=0)
@@ -442,7 +447,6 @@
             own_cube[number] = own_cube[number] - 2.0 * back_buf[i]
         for o in range(OWN):
             finish(o, own_cube[o])
-        pltpu.make_async_copy(out_buf.at[g], purified.at[g], out_sem.at[g]).start()
         return 0
 
     lax.fori_loop(0, OWN, rows, 0, unroll=2)
@@ -520,14 +524,18 @@
     far_ahead = lax.ppermute(far_m, AXES, from_direction(2))
     far_behind = lax.ppermute(far_p, AXES, from_direction(0))
     beside_own = lax.ppermute(beside_own, AXES, from_direction(1))
+    late_p = call(
+        functools.partial(late_kernel, (4,)), "late", blocks(10),
+        [SMEM, VMEM, ANY], VMEM, [], 0, 1,
+    )(tab, dens, beside_own)
     tab, wide, square = call(
         local_kernel, "local",
         (table, wides(OWN * SLOTS), blocks(OWN * SLOTS)),
         [SMEM, VMEM, SMEM, ANY], (SMEM,) + (VMEM,) * 2, [wide_scratch()], 400, 9,
-    )(pattern.T, dens, tab, beside_own)
-    late_m, late_p, beside = call(
-        late_kernel, "late", (blocks(10), blocks(10), blocks(10)),
-        [SMEM, VMEM, ANY], (VMEM,) * 3, [], 0, 3,
+    )(pattern.T, dens, tab, late_p)
+    late_m, beside = call(
+        functools.partial(late_kernel, (3, 1)), "later", (blocks(10), blocks(10)),
+        [SMEM, VMEM, ANY], (VMEM,) * 2, [], 0, 2,
     )(tab, dens, square)
     pair_low, pair_high = call(
         second_kernel, "second", (blocks(8), blocks(8)),

time: 88.7 us -> 88.5 us (level)
  transfers between devices with their start and end apart: 10 -> 10, of which waited for: 2 -> 2; matrix products, arithmetic and copies ran while one was open for 0% -> 0% of each run, Pallas kernels for 24% -> 25%
where the time goes in v5:
time: 88.5 us; the launch traced here: 88.3 us
  Pallas kernels  34.3 us (39%)
  starting transfers between devices  26.5 us (30%)
  blocking collectives  20.7 us (23%)
  waiting for transfers between devices  4.39 us (5%)
  local copies, waits for them, and re-layouts  1.38 us (2%)
    all_to_all x1, blocking collectives, body(): lines = lax.all_to_all(line, AXES, 0, 0, tiled=True)  20.7 us
    pallas_call x1, Pallas kernels, body(): call(final_kernel, 'final', (blocks(OWN, SLOTS), jax.ShapeDtypeStruct((N_...  8.24 us
    pallas_call x1, Pallas kernels, body(): call(local_kernel, 'local', (table, wides(OWN * SLOTS), blocks(OWN * SLOT...  8.15 us
    pallas_call x1, Pallas kernels, body(): call(pair_kernel, 'pair', (wides(16), wides(N_PAIR), blocks(OWN * SLOTS),...  6.46 us
    ppermute x1, starting transfers between devices, body(): far_ahead = lax.ppermute(far_m, AXES, from_direction(2))  6.26 us
    pallas_call x1, Pallas kernels, body(): call(first_kernel, 'first', (table, blocks(10), blocks(10), blocks(8), bl...  4.29 us
    ppermute x1, starting transfers between devices, body(): near_ahead = lax.ppermute(near_m, AXES, from_direction(7))  4.29 us
    ppermute x1, starting transfers between devices, body(): pair_low_in = lax.ppermute(pair_low, AXES, from_direction(6))  3.87 us
  transfers between devices with their start and end apart: 10, of which 2 were waited for; matrix products, arithmetic and copies ran while one was open for 0% of the time, Pallas kernels for 25%

profile of v5, /device:TPU:1, one launch (start us, length us, event | category | flops | bytes accessed | tf_op | source)
XLA Modules:
  0.0 88.3 jit_solution(16318844686147070100)
XLA Ops:
  0.6 4.3 %first.1 = (s32[344]{0:T(512)}, f32[10,128,128]{2,1,0:T(8,128)}, f32[10,128,128]{2,1,0:T(8,128)}, f32[8,128,128]{2,1,0:T(8,128)}, f32[8,128,128]{2,1,0:T(8,128)}, /*index=5*/f32[2,128,128]{2,1,0:T(8,128)}) custom-call(s32[12,512]{1,0:T(8,128)} %bitcast.13, f32[48,128,128]{2,1,0:T(8,128)} %bitcast.5), custom_call_target="tpu_custom_call" | custom-call | bytes 10485760 | tf_op jit(solution)/shard_map/first/pallas_call | solution.py:517
  4.9 2.8 %collective-permute-start = (f32[2,128,128]{2,1,0:T(8,128)}, f32[2,128,128]{2,1,0:T(8,128)S(1)}, u32[]{:S(2)}, u32[]{:S(2)}) collective-permute-start(f32[2,128,128]{2,1,0:T(8,128)} %get-tuple-element.28), channel_id=1, source_target_pairs={{120,0},{121,1},{122,2},{123,3},{124,4},{125,5},{126,6},{127,7},{1... | collective-permute-start | bytes 393224 | tf_op jit(solution)/shard_map/ppermute | solution.py:526
  7.7 3.7 %collective-permute-start.1 = (f32[10,128,128]{2,1,0:T(8,128)}, f32[10,128,128]{2,1,0:T(8,128)S(1)}, u32[]{:S(2)}, u32[]{:S(2)}) collective-permute-start(f32[10,128,128]{2,1,0:T(8,128)} %get-tuple-element.32), channel_id=1, source_target_pairs={{15,0},{8,1},{9,2},{10,3},{11,4},{12,5},{13,6},{14,7},{7,8},{0,9},... | collective-permute-start | bytes 1966088 | tf_op jit(solution)/shard_map/ppermute | solution.py:523
  11.4 4.3 %collective-permute-start.2 = (f32[10,128,128]{2,1,0:T(8,128)}, f32[10,128,128]{2,1,0:T(8,128)S(1)}, u32[]{:S(2)}, u32[]{:S(2)}) collective-permute-start(f32[10,128,128]{2,1,0:T(8,128)} %get-tuple-element.33), channel_id=1, source_target_pairs={{9,0},{10,1},{11,2},{12,3},{13,4},{14,5},{15,6},{8,7},{1,8},{2,9},... | collective-permute-start | bytes 1966088 | tf_op jit(solution)/shard_map/ppermute | solution.py:522
  15.7 0.0 collective-permute-start.3
  15.7 6.3 %collective-permute-start.4 = (f32[8,128,128]{2,1,0:T(8,128)}, f32[8,128,128]{2,1,0:T(8,128)S(1)}, u32[]{:S(2)}, u32[]{:S(2)}) collective-permute-start(f32[8,128,128]{2,1,0:T(8,128)} %get-tuple-element.35), channel_id=1, source_target_pairs={{121,0},{122,1},{123,2},{124,3},{125,4},{126,5},{127,6},{120,7},{1... | collective-permute-start | bytes 1572872 | tf_op jit(solution)/shard_map/ppermute | solution.py:524
  22.0 0.0 collective-permute-done.refs_0_.beside
  22.0 0.7 copy-done.2
  22.7 0.6 late.1.after
  23.3 0.1 collective-permute-start.7
  23.4 8.2 %local.1 = (s32[344]{0:T(512)S(1)}, bf16[48,128,256]{2,1,0:T(8,128)(2,1)S(1)}, f32[48,128,128]{2,1,0:T(8,128)S(1)}) custom-call(s32[12,512]{1,0:T(8,128)S(1)} %bitcast.14, f32[48,128,128]{2,1,0:T(8,128)S(1)} %bitcast.7, s32[344]{0:T(512)S(1)} %copy-done.2, f32[10,128,128]{2,1,0:T(8,128)S(1)} %late.1.after), custom_call_target="tpu_custom_call" | custom-call | flops 6710886400 | bytes 9437184 | tf_op jit(solution)/shard_map/local/pallas_call | solution.py:531
  31.5 0.6 later.1
  32.2 2.2 %collective-permute-done.1.near_m.behind = f32[10,128,128]{2,1,0:T(8,128)S(1)} collective-permute-done((f32[10,128,128]{2,1,0:T(8,128)}, f32[10,128,128]{2,1,0:T(8,128)S(1)}, u32[]{:S(2)}, u32[]{:S(2)}) %collective-permute-start.1) | collective-permute-done | bytes 655392 | tf_op jit(solution)/shard_map/ppermute | solution.py:523
  34.4 3.2 %collective-permute-start.9 = (f32[10,128,128]{2,1,0:T(8,128)S(1)}, f32[10,128,128]{2,1,0:T(8,128)S(1)}, u32[]{:S(2)}, u32[]{:S(2)}) collective-permute-start(f32[10,128,128]{2,1,0:T(8,128)S(1)} %get-tuple-element.36.after), channel_id=1, source_target_pairs={{120,0},{121,1},{122,2},{123,3},{124,4},{125,5},{126,6},{127,7},{1... | collective-permute-start | bytes 1966088 | tf_op jit(solution)/shard_map/ppermute | solution.py:548
  37.7 2.1 %collective-permute-done.2.near_p.ahead = f32[10,128,128]{2,1,0:T(8,128)S(1)} collective-permute-done((f32[10,128,128]{2,1,0:T(8,128)}, f32[10,128,128]{2,1,0:T(8,128)S(1)}, u32[]{:S(2)}, u32[]{:S(2)}) %collective-permute-start.2) | collective-permute-done | bytes 655392 | tf_op jit(solution)/shard_map/ppermute | solution.py:522
  39.8 2.0 %collective-permute-start.8 = (f32[10,128,128]{2,1,0:T(8,128)S(1)}, f32[10,128,128]{2,1,0:T(8,128)S(1)}, u32[]{:S(2)}, u32[]{:S(2)}) collective-permute-start(f32[10,128,128]{2,1,0:T(8,128)S(1)} %get-tuple-element.37.also), channel_id=1, source_target_pairs={{1,0},{2,1},{3,2},{4,3},{5,4},{6,5},{7,6},{0,7},{9,8},{10,9},{11,1... | collective-permute-start | bytes 1966088 | tf_op jit(solution)/shard_map/ppermute | solution.py:544
  41.8 0.6 second.1
  42.5 0.0 collective-permute-done.3.far_m
  42.5 3.9 %collective-permute-start.5 = (f32[8,128,128]{2,1,0:T(8,128)S(1)}, f32[8,128,128]{2,1,0:T(8,128)S(1)}, u32[]{:S(2)}, u32[]{:S(2)}) collective-permute-start(f32[8,128,128]{2,1,0:T(8,128)S(1)} %get-tuple-element.40), channel_id=1, source_target_pairs={{8,0},{9,1},{10,2},{11,3},{12,4},{13,5},{14,6},{15,7},{0,8},{1,9},... | collective-permute-start | bytes 1572872 | tf_op jit(solution)/shard_map/ppermute | solution.py:546
  46.3 0.3 collective-permute-start.6
  46.6 2.9 %early.1 = (bf16[16,128,256]{2,1,0:T(8,128)(2,1)S(1)}, bf16[24,128,256]{2,1,0:T(8,128)(2,1)S(1)}, f32[48,128,128]{2,1,0:T(8,128)S(1)}) custom-call(s32[344]{0:T(512)S(1)} %get-tuple-element.29.tab, bf16[48,128,256]{2,1,0:T(8,128)(2,1)S(1)} %get-tuple-element.30.wide, f32[48,128,128]{2,1,0:T(8,128)S(1)} %get-tuple-element.31.refs_0_.square_in, ...), custom_call_target="tpu_custom_call" | custom-call | tf_op jit(solution)/shard_map/early/pallas_call | solution.py:549
  49.5 0.0 collective-permute-done.5.low
  49.5 0.0 slice-start.2
  49.6 6.5 %pair.1 = (bf16[16,128,256]{2,1,0:T(8,128)(2,1)S(1)}, bf16[10,128,256]{2,1,0:T(8,128)(2,1)S(1)}, f32[48,128,128]{2,1,0:T(8,128)S(1)}, f32[48,128,128]{2,1,0:T(8,128)S(1)}) custom-call(s32[344]{0:T(512)S(1)} %get-tuple-element.29.tab, bf16[48,128,256]{2,1,0:T(8,128)(2,1)S(1)} %get-tuple-element.30.wide, f32[48,128,128]{2,1,0:T(8,128)S(1)} %get-tuple-element.39.square_in, ...), custom_call_target="tpu_custom_call" | custom-call | tf_op jit(solution)/shard_map/pair/pallas_call | solution.py:555
  56.0 0.0 collective-permute-done.7.ref
  56.0 0.0 slice-start.3
  56.0 2.4 %behind.1 = (bf16[10,128,256]{2,1,0:T(8,128)(2,1)S(1)}, f32[48,128,128]{2,1,0:T(8,128)S(1)}, f32[48,128,128]{2,1,0:T(8,128)S(1)}) custom-call(s32[344]{0:T(512)S(1)} %get-tuple-element.29.tab, bf16[48,128,256]{2,1,0:T(8,128)(2,1)S(1)} %get-tuple-element.30.wide, f32[48,128,128]{2,1,0:T(8,128)S(1)} %get-tuple-element.45.square_in, ...), custom_call_target="tpu_custom_call" | custom-call | tf_op jit(solution)/shard_map/behind/pallas_call | solution.py:561
  58.5 0.0 collective-permute-done.9.beside
  58.5 8.2 %final.1 = (f32[4,12,128,128]{3,2,1,0:T(8,128)}, f32[128,128]{1,0:T(8,128)S(1)}) custom-call(s32[344]{0:T(512)S(1)} %get-tuple-element.29.tab, bf16[48,128,256]{2,1,0:T(8,128)(2,1)S(1)} %get-tuple-element.30.wide, bf16[16,128,256]{2,1,0:T(8,128)(2,1)S(1)} %get-tuple-element.38.own_early, bf16[16,128,256]{2,1,0:T(8,128)(2,1)S(1)} %get-tuple-element.42.own_late, ...), custom_call_target="tpu_custom_call" | custom-call | flops 3355443200 | bytes 31457280 | tf_op jit(solution)/shard_map/final/pallas_call | solution.py:566
  66.8 20.7 %all_to_all.9 = f32[128,1,128]{2,1,0:T(1,128)S(1)} all-to-all(f32[128,1,128]{2,1,0:T(1,128)S(1)} %bitcast.12), channel_id=1, replica_groups=mesh['row'=16,'col'=8] {'row','col'}, dimensions={0} | all-to-all | bytes 131072 | tf_op jit(solution)/shard_map/all_to_all | solution.py:578
  87.5 0.2 reduce_sum.9
  87.7 0.7 mul.8
  (16 shorter events, 0.0 us)
Async XLA Ops:
  0.6 21.4 %copy-start = (f32[4,12,128,128]{3,2,1,0:T(8,128)S(1)}, f32[4,12,128,128]{3,2,1,0:T(8,128)}, u32[]{:S(2)}) copy-start(f32[4,12,128,128]{3,2,1,0:T(8,128)} %param.3) | copy-start | bytes 9437188
  0.6 22.7 %copy-start.1 = (s32[512,12]{0,1:T(8,128)S(1)}, s32[512,12]{0,1:T(8,128)}, u32[]{:S(2)}) copy-start(s32[512,12]{0,1:T(8,128)} %param.4) | copy-start | bytes 73732
  4.9 17.0 %collective-permute-start = (f32[2,128,128]{2,1,0:T(8,128)}, f32[2,128,128]{2,1,0:T(8,128)S(1)}, u32[]{:S(2)}, u32[]{:S(2)}) collective-permute-start(f32[2,128,128]{2,1,0:T(8,128)} %get-tuple-element.28), channel_id=1, source_target_pairs={{120,0},{121,1},{122,2},{123,3},{124,4},{125,5},{126,6},{127,7},{1... | collective-permute-start | bytes 393224 | tf_op jit(solution)/shard_map/ppermute | solution.py:526
  7.7 26.7 %collective-permute-start.1 = (f32[10,128,128]{2,1,0:T(8,128)}, f32[10,128,128]{2,1,0:T(8,128)S(1)}, u32[]{:S(2)}, u32[]{:S(2)}) collective-permute-start(f32[10,128,128]{2,1,0:T(8,128)} %get-tuple-element.32), channel_id=1, source_target_pairs={{15,0},{8,1},{9,2},{10,3},{11,4},{12,5},{13,6},{14,7},{7,8},{0,9},... | collective-permute-start | bytes 1966088 | tf_op jit(solution)/shard_map/ppermute | solution.py:523
  11.4 28.4 %collective-permute-start.2 = (f32[10,128,128]{2,1,0:T(8,128)}, f32[10,128,128]{2,1,0:T(8,128)S(1)}, u32[]{:S(2)}, u32[]{:S(2)}) collective-permute-start(f32[10,128,128]{2,1,0:T(8,128)} %get-tuple-element.33), channel_id=1, source_target_pairs={{9,0},{10,1},{11,2},{12,3},{13,4},{14,5},{15,6},{8,7},{1,8},{2,9},... | collective-permute-start | bytes 1966088 | tf_op jit(solution)/shard_map/ppermute | solution.py:522
  15.7 26.7 %collective-permute-start.3 = (f32[8,128,128]{2,1,0:T(8,128)}, f32[8,128,128]{2,1,0:T(8,128)S(1)}, u32[]{:S(2)}, u32[]{:S(2)}) collective-permute-start(f32[8,128,128]{2,1,0:T(8,128)} %get-tuple-element.34), channel_id=1, source_target_pairs={{127,0},{120,1},{121,2},{122,3},{123,4},{124,5},{125,6},{126,7},{2... | collective-permute-start | bytes 1572872 | tf_op jit(solution)/shard_map/ppermute | solution.py:525
  15.7 30.6 %collective-permute-start.4 = (f32[8,128,128]{2,1,0:T(8,128)}, f32[8,128,128]{2,1,0:T(8,128)S(1)}, u32[]{:S(2)}, u32[]{:S(2)}) collective-permute-start(f32[8,128,128]{2,1,0:T(8,128)} %get-tuple-element.35), channel_id=1, source_target_pairs={{121,0},{122,1},{123,2},{124,3},{125,4},{126,5},{127,6},{120,7},{1... | collective-permute-start | bytes 1572872 | tf_op jit(solution)/shard_map/ppermute | solution.py:524
  22.0 0.7 copy-start.2
  23.3 32.7 %collective-permute-start.7 = (f32[10,128,128]{2,1,0:T(8,128)S(1)}, f32[10,128,128]{2,1,0:T(8,128)S(1)}, u32[]{:S(2)}, u32[]{:S(2)}) collective-permute-start(f32[10,128,128]{2,1,0:T(8,128)S(1)} %late.1.after), channel_id=1, source_target_pairs={{7,0},{0,1},{1,2},{2,3},{3,4},{4,5},{5,6},{6,7},{15,8},{8,9},{9,10... | collective-permute-start | bytes 1966088 | tf_op jit(solution)/shard_map/ppermute | solution.py:545
  34.4 24.0 %collective-permute-start.9 = (f32[10,128,128]{2,1,0:T(8,128)S(1)}, f32[10,128,128]{2,1,0:T(8,128)S(1)}, u32[]{:S(2)}, u32[]{:S(2)}) collective-permute-start(f32[10,128,128]{2,1,0:T(8,128)S(1)} %get-tuple-element.36.after), channel_id=1, source_target_pairs={{120,0},{121,1},{122,2},{123,3},{124,4},{125,5},{126,6},{127,7},{1... | collective-permute-start | bytes 1966088 | tf_op jit(solution)/shard_map/ppermute | solution.py:548
  39.8 18.7 %collective-permute-start.8 = (f32[10,128,128]{2,1,0:T(8,128)S(1)}, f32[10,128,128]{2,1,0:T(8,128)S(1)}, u32[]{:S(2)}, u32[]{:S(2)}) collective-permute-start(f32[10,128,128]{2,1,0:T(8,128)S(1)} %get-tuple-element.37.also), channel_id=1, source_target_pairs={{1,0},{2,1},{3,2},{4,3},{5,4},{6,5},{7,6},{0,7},{9,8},{10,9},{11,1... | collective-permute-start | bytes 1966088 | tf_op jit(solution)/shard_map/ppermute | solution.py:544
  42.5 7.1 %collective-permute-start.5 = (f32[8,128,128]{2,1,0:T(8,128)S(1)}, f32[8,128,128]{2,1,0:T(8,128)S(1)}, u32[]{:S(2)}, u32[]{:S(2)}) collective-permute-start(f32[8,128,128]{2,1,0:T(8,128)S(1)} %get-tuple-element.40), channel_id=1, source_target_pairs={{8,0},{9,1},{10,2},{11,3},{12,4},{13,5},{14,6},{15,7},{0,8},{1,9},... | collective-permute-start | bytes 1572872 | tf_op jit(solution)/shard_map/ppermute | solution.py:546
  46.3 3.2 %collective-permute-start.6 = (f32[8,128,128]{2,1,0:T(8,128)S(1)}, f32[8,128,128]{2,1,0:T(8,128)S(1)}, u32[]{:S(2)}, u32[]{:S(2)}) collective-permute-start(f32[8,128,128]{2,1,0:T(8,128)S(1)} %get-tuple-element.41), channel_id=1, source_target_pairs={{8,0},{9,1},{10,2},{11,3},{12,4},{13,5},{14,6},{15,7},{0,8},{1,9},... | collective-permute-start | bytes 1572872 | tf_op jit(solution)/shard_map/ppermute | solution.py:547
  46.6 11.9 %slice-start = ((s8[14155776]{0:T(1024)(128)(4,1)}), s8[4194304]{0:T(1024)(128)(4,1)S(1)}, s32[]{:S(2)}) async-start(s8[14155776]{0:T(1024)(128)(4,1)} %bitcast.10), calls=%async_computation.1 | async-start | bytes 8388608
  46.6 11.9 %slice-start.1 = ((s8[14155776]{0:T(1024)(128)(4,1)}), s8[4194304]{0:T(1024)(128)(4,1)S(1)}, s32[]{:S(2)}) async-start(s8[14155776]{0:T(1024)(128)(4,1)} %bitcast.10), calls=%async_computation.2 | async-start | bytes 8388608
  49.5 9.0 %slice-start.2 = ((s8[14155776]{0:T(1024)(128)(4,1)}), s8[4194304]{0:T(1024)(128)(4,1)S(1)}, s32[]{:S(2)}) async-start(s8[14155776]{0:T(1024)(128)(4,1)} %bitcast.10), calls=%async_computation.3 | async-start | bytes 8388608
  56.0 2.5 %slice-start.3 = ((s8[14155776]{0:T(1024)(128)(4,1)}), s8[1572864]{0:T(1024)(128)(4,1)S(1)}, s32[]{:S(2)}) async-start(s8[14155776]{0:T(1024)(128)(4,1)} %bitcast.10), calls=%async_computation.4 | async-start | bytes 3145728
